TPU v7x, 512 devices: a whole 4x4x16 slice. The times are simulated.
512 devices in a mesh: seq: 16 (over x, y), fsdp: 32 (over z, core).
Axes of the slice: x: 4, y: 4, z: 16, core: 2. Of those that a mesh axis runs over, the one named last changes fastest.
Arguments:
- activations: bfloat16 [32, 4096, 2048], P('fsdp', 'seq'), may hold values from -6 to 6
- proj_weight: bfloat16 [2048, 2048], P('fsdp'), may hold values from -0.125 to 0.125
- gate_weight: bfloat16 [2048, 8], P('fsdp'), may hold values from -7.9549513 to 7.9549513
- forget_bias: float32 [4], replicated, may hold values from 5.2 to 11.5
- accepted: int32 [32], P('fsdp'), may hold values from 1024 to 4096, as said below
Outputs:
- hidden_out: bfloat16 [32, 4096, 1024], P('fsdp', 'seq')
Inputs may be any that keep to these rules, and one draw needn't show every extreme that they name: Some sequence has accepted length 4096.
All inputs are finite; a program needn't handle non-finite values.
Results may differ from a plain program's by a relative error of at most 0.0074.
Values may be sent and summed in bfloat16 or wider, within the bound.
No kernel may reach another device: no remote copies, remote signals or barrier semaphores. Data moves between devices by JAX's collectives and lax.ppermute only.
A program may use at most 64 MiB of HBM per device.

v0:
```python
import jax
import jax.numpy as jnp
from jax import lax
from jax.sharding import PartitionSpec as P

H = 4
DK = 128
DV = 256


lowest = -1e30


def prefix_2(part, axis, combine, identity):
    place = lax.axis_index(axis)
    gathered = jax.tree.map(lambda a: lax.all_gather(a, axis), part)
    state = jax.tree.map(lambda a, e: jnp.zeros_like(a) + jnp.asarray(e, a.dtype), part, identity)

    def one(hop, state):
        return combine(
            state, jax.tree.map(lambda a: lax.dynamic_index_in_dim(a, hop, 0, False), gathered)
        )

    return lax.fori_loop(0, place, one, state)


def combine(earlier, later):
    total_a, top_a, memory_a, normal_a = earlier
    total_b, top_b, memory_b, normal_b = later
    top_log = jnp.maximum(total_b + top_a, top_b)
    scale_a = jnp.exp(total_b + top_a - top_log)
    scale_b = jnp.exp(top_b - top_log)
    return (
        total_a + total_b,
        top_log,
        scale_a[:, None, None] * memory_a + scale_b[:, None, None] * memory_b,
        scale_a[:, None] * normal_a + scale_b[:, None] * normal_b,
    )


def gate_logs(gate_pre, forget_bias, live_rows):
    head_count = forget_bias.shape[0]
    input_pre = gate_pre[:, :head_count]
    forget_pre = gate_pre[:, head_count:] + forget_bias
    log_forget = jnp.where(live_rows[:, None], jax.nn.log_sigmoid(forget_pre), 0.0)
    log_input = jnp.where(live_rows[:, None], input_pre, lowest)
    return (log_forget, log_input)


def summarize(key_rows, value_entries, log_forget, log_input, live_rows):
    decay_sum = jnp.cumsum(log_forget, axis=0)
    total_log = decay_sum[-1]
    tail_log = total_log[None, :] - decay_sum + log_input
    top_log = jnp.max(tail_log, axis=0)
    scaling = jnp.where(live_rows[:, None], jnp.exp(tail_log - top_log[None, :]), 0.0)
    weighted_values = key_rows.astype(jnp.float32) * scaling[:, :, None]
    memory_matrix = jnp.einsum(
        "lpz,lpu->pzu",
        weighted_values,
        value_entries.astype(jnp.float32),
        precision=lax.Precision.HIGHEST,
    )
    normal = jnp.sum(weighted_values, axis=0)
    return (total_log, top_log, memory_matrix, normal)


def block_output(
    query_rows,
    key_rows,
    value_entries,
    log_forget,
    log_input,
    live_rows,
    top_in,
    incoming_memory,
    normal_in,
):
    row_count = query_rows.shape[0]
    rescale_factor = query_rows.shape[2] ** (-0.5)
    decay_sum = jnp.cumsum(log_forget, axis=0).T
    log_weight = decay_sum[:, :, None] - decay_sum[:, None, :] + log_input.T[:, None, :]
    causal = jnp.arange(row_count)[:, None] >= jnp.arange(row_count)[None, :]
    log_weight = jnp.where(causal[None], log_weight, lowest)
    carried = decay_sum + top_in[:, None]
    top_row = jnp.maximum(jnp.max(log_weight, axis=2), carried)
    weights = jnp.exp(log_weight - top_row[:, :, None])
    carry_scale = jnp.exp(carried - top_row)
    scores = (
        jnp.einsum("thk,shk->hts", query_rows, key_rows, preferred_element_type=jnp.float32)
        * rescale_factor
    )
    products = weights * scores
    query_broadened = query_rows.astype(jnp.float32)
    denominator = (
        jnp.sum(products, axis=2)
        + carry_scale
        * jnp.einsum("thk,hk->ht", query_broadened, normal_in, precision=lax.Precision.HIGHEST)
        * rescale_factor
    )
    numerator = jnp.einsum(
        "hts,shv->thv",
        products.astype(jnp.bfloat16),
        value_entries,
        preferred_element_type=jnp.float32,
    )
    numerator = (
        numerator
        + carry_scale.T[:, :, None]
        * jnp.einsum(
            "ilq,lqg->ilg", query_broadened, incoming_memory, precision=lax.Precision.HIGHEST
        )
        * rescale_factor
    )
    divisor = jnp.maximum(jnp.abs(denominator), 1.0).T
    result = jnp.where(live_rows[:, None, None], numerator / divisor[:, :, None], 0.0)
    return result.reshape(row_count, -1)


def per_device(activations, proj_weight, gate_weight, forget_bias, accepted):
    token_rows = activations[0]
    row_count = token_rows.shape[0]
    whole_proj, whole_gate = (
        lax.all_gather(proj_weight, "fsdp", axis=0, tiled=True),
        lax.all_gather(gate_weight, "fsdp", axis=0, tiled=True),
    )
    projected = jnp.dot(token_rows, whole_proj, preferred_element_type=jnp.float32).astype(
        jnp.bfloat16
    )
    gate_pre = jnp.dot(token_rows, whole_gate, preferred_element_type=jnp.float32)
    own_index = lax.axis_index("seq")
    positions = own_index * row_count + jnp.arange(row_count, dtype=jnp.int32)
    live_rows = positions < accepted[0]
    log_forget, log_input = gate_logs(gate_pre, forget_bias, live_rows)
    query_rows = projected[:, : H * DK].reshape(row_count, H, DK)
    key_rows = projected[:, H * DK : 2 * H * DK].reshape(row_count, H, DK)
    value_entries = projected[:, 2 * H * DK :].reshape(row_count, H, DV)
    summary = summarize(key_rows, value_entries, log_forget, log_input, live_rows)
    identity = (
        jnp.zeros((H,), jnp.float32),
        jnp.full((H,), lowest, jnp.float32),
        jnp.zeros((H, DK, DV), jnp.float32),
        jnp.zeros((H, DK), jnp.float32),
    )
    prefix = prefix_2(summary, "seq", combine, identity)
    top_in, incoming_memory, normal_in = (prefix[1], prefix[2], prefix[3])
    output = block_output(
        query_rows,
        key_rows,
        value_entries,
        log_forget,
        log_input,
        live_rows,
        top_in,
        incoming_memory,
        normal_in,
    )
    return output.astype(jnp.bfloat16)[None]


def solution(mesh):
    placed = (P("fsdp", "seq", None), P("fsdp", None), P("fsdp", None), P(), P("fsdp"))
    return jax.shard_map(
        per_device, mesh=mesh, in_specs=placed, out_specs=P("fsdp", "seq", None), check_vma=False
    )
```

profile of v0, /device:TPU:30, one launch (start us, length us, event | category | flops | bytes accessed | tf_op | source)
XLA Modules:
  0.0 216.4 jit_solution(10821680505047758857)
XLA Ops:
  6.5 0.7 all-gather.7.cloned.1.call-update
  8.0 36.7 %all-gather.2 = bf16[32,64,8]{1,2,0:T(8,128)(2,1)S(1)} all-gather(bf16[1,64,8]{1,2,0:T(8,128)(2,1)} %bitcast.154), channel_id=1, replica_groups=mesh['seq'=16,'fsdp'=32] {'fsdp'}, dimensions={0}, use_global_device_ids=true | all-gather | bytes 33792 | tf_op jit(solution)/shard_map/all_gather | solution.py:124
  44.7 0.1 reshape.123
  44.8 0.4 fusion.13
  45.2 0.8 fusion.31
  46.0 1.2 reduce-window.6
  47.2 0.1 slice.34
  47.3 0.1 copy.36
  47.4 0.1 copy.37
  47.6 0.2 slice_reduce_fusion
  47.8 0.2 fusion.40
  48.0 0.1 exponential_select_fusion
  48.0 45.1 %all-gather.7.cloned.1.call-done = bf16[2048,2048]{1,0:T(8,128)(2,1)} async-done(((bf16[64,2048]{1,0:T(8,128)(2,1)}), bf16[2048,2048]{1,0:T(8,128)(2,1)}) %all-gather.7.cloned.1.call-update) | async-done | bytes 8388624 | tf_op jit(solution)/shard_map/all_gather | solution.py:123
  93.1 5.7 %convolution_convert_fusion = bf16[256,2048]{1,0:T(8,128)(2,1)S(1)} fusion(bf16[2048,2048]{1,0:T(8,128)(2,1)} %all-gather.7.cloned.1.call-done, bf16[1,256,2048]{2,1,0:T(8,128)(2,1)S(1)} %copy-done), kind=kOutput, calls=%fused_computation.12 | convolution fusion | flops 2148007936 | bytes 10485760 | tf_op jit(solution)/shard_map/dot_general | solution.py:126
  98.9 1.0 copy-done.1
  100.0 0.1 copy.57
  100.1 0.2 copy.56
  100.3 1.4 fusion.18
  101.8 1.3 dynamic-slice
  103.8 0.2 dynamic-update-slice
  104.0 35.3 %all-reduce = f32[64]{0:T(128)S(1)} all-reduce(f32[64]{0:T(128)S(1)} %dynamic-update-slice), channel_id=2, replica_groups=mesh['seq'=16,'fsdp'=32] {'seq'}, use_global_device_ids=true, to_apply=%add | all-reduce | flops 64 | bytes 512
  139.3 0.1 reshape.117
  139.4 0.2 copy.55
  139.6 19.6 %all-gather.3 = f32[16,1,4]{2,1,0:T(1,128)S(1)} all-gather(f32[1,1,4]{2,1,0:T(1,128)S(1)} %bitcast.152), channel_id=1, replica_groups=mesh['seq'=16,'fsdp'=32] {'seq'}, dimensions={0}, use_global_device_ids=true | all-gather | bytes 272 | tf_op jit(solution)/shard_map/all_gather | solution.py:16
  159.3 0.4 fusion.16
  159.6 1.0 multiply_reduce_fusion
  160.7 23.8 %all_gather.35 = f32[16,4,128]{2,1,0:T(4,128)S(1)} all-gather(f32[1,4,128]{2,1,0:T(4,128)S(1)} %bitcast.151), channel_id=1, replica_groups=mesh['seq'=16,'fsdp'=32] {'seq'}, dimensions={0}, use_global_device_ids=true | all-gather | bytes 34816 | tf_op jit(solution)/shard_map/all_gather | solution.py:16
  184.6 21.8 %while.16 = (s32[]{:T(128)}, f32[4]{0:T(128)S(1)}, f32[4,128,256]{2,1,0:T(8,128)S(1)}, f32[4,128]{1,0:T(4,128)S(1)}, s32[]{:T(128)}, /*index=5*/f32[16,4]{1,0:T(...) while((s32[]{:T(128)}, f32[4]{0:T(128)S(1)}, ...), condition=%wide.region_6.7_spmd, body=%wide.region_5.6_spmd.sunk | while | flops 394773 | bytes 1579375 | solution.py:24
  184.6 0.1 fusion.55
  184.7 1.3 fusion.54
  186.1 0.1 fusion.55
  186.2 1.3 fusion.54
  187.5 0.1 fusion.55
  187.6 1.3 fusion.54
  189.0 0.1 fusion.55
  189.1 1.3 fusion.54
  190.4 0.1 fusion.55
  190.5 1.3 fusion.54
  191.9 0.1 fusion.55
  192.0 1.3 fusion.54
  193.4 0.1 fusion.55
  193.4 1.3 fusion.54
  194.8 0.1 fusion.55
  194.9 1.3 fusion.54
  196.3 0.1 fusion.55
  196.4 1.3 fusion.54
  197.7 0.1 fusion.55
  197.8 1.3 fusion.54
  199.2 0.1 fusion.55
  199.3 1.3 fusion.54
  200.6 0.1 fusion.55
  200.7 1.3 fusion.54
  202.1 0.1 fusion.55
  202.2 1.3 fusion.54
  203.5 0.1 fusion.55
  203.6 1.3 fusion.54
  205.0 0.1 fusion.55
  205.1 1.3 fusion.54
  206.4 0.3 fusion.22
  206.8 0.6 fusion.43
  207.4 0.3 convolution_bitcast_fusion.1
  207.7 0.1 fusion.39
  207.8 0.7 fusion.12
  208.5 1.0 copy.49
  (53 shorter events, 1.0 us)
Async XLA Ops:
  6.5 38.3 %copy-start = (bf16[1,256,2048]{2,1,0:T(8,128)(2,1)S(1)}, bf16[1,256,2048]{2,1,0:T(8,128)(2,1)}, u32[]{:S(2)}) copy-start(bf16[1,256,2048]{2,1,0:T(8,128)(2,1)} %param.7) | copy-start | bytes 3145732
  6.5 86.6 %all-gather.7.cloned.1.call-start = ((), (), s32[]{:S(2)}) async-start(), calls=%async_computation | async-start | bytes 8650752 | tf_op jit(solution)/shard_map/all_gather | solution.py:123
  7.3 177.2 %all-gather.9.cloned.1.call-start = ((), (), s32[]{:S(2)}) async-start(), calls=%async_computation.1 | async-start | bytes 8912896 | tf_op jit(solution)/shard_map/all_gather | solution.py:16
  98.8 1.1 copy-start.1
Sparse Core Ops, SparseCore 0:
  9.5 83.6 all-gather.6
  101.9 80.9 all-gather.8
where the time goes:
time: 217 us; the launch traced here: 216 us
  blocking collectives  115 us (53%)
  waiting for transfers between devices  45.8 us (21%)
  other arithmetic  25.3 us (12%)
  between operations  14.9 us (7%)
  matrix products  9.46 us (4%)
  local copies, waits for them, and re-layouts  5 us (2%)
    all_gather x1, waiting for transfers between devices, per_device(): lax.all_gather(proj_weight, 'fsdp', axis=0, tiled=True)  45.1 us
    all_gather x2, blocking collectives, prefix_2(): gathered = jax.tree.map(lambda a: lax.all_gather(a, axis), part)  43.4 us
    all_gather x1, blocking collectives, per_device(): lax.all_gather(gate_weight, 'fsdp', axis=0, tiled=True)  36.7 us
    unnamed x1, blocking collectives  35.3 us
    add x15, other arithmetic, combine(): scale_a[:, None, None] * memory_a + scale_b[:, None, None] * memory_b  19.6 us
    dot_general x1, matrix products, per_device(): jnp.dot(token_rows, whole_proj, preferred_element_type=jnp.float32)  5.71 us
  transfers between devices with their start and end apart: 2, of which 1 were waited for; matrix products, arithmetic and copies ran while one was open for 3% of the time, Pallas kernels for 0%

commit v1 on v0

v1 whole, which is shorter than its diff:
```python
import functools

import jax
import jax.numpy as jnp
from jax import lax
from jax.experimental import pallas as pl
from jax.experimental.pallas import tpu as pltpu
from jax.sharding import Mesh
from jax.sharding import PartitionSpec as P

D = 2048
H = 4
DK = 128
DV = 256
TOK = 256
NX, NY, NZ, NC = 4, 4, 16, 2
QUAD = NY * TOK
HALF = D // (NZ * NC)
PIECE = HALF + 8
EXT = DV + 128
lowest = -1e30


def dot(a, b, contract=((1,), (0,))):
    return lax.dot_general(a, b, (contract, ((), ())), preferred_element_type=jnp.float32)


def split3(value):
    high = value.astype(jnp.bfloat16).astype(jnp.float32)
    rest = value - high
    middle = rest.astype(jnp.bfloat16).astype(jnp.float32)
    return high, middle, rest - middle


def scan_lanes(row, combine, neutral):
    size, step = row.shape[1], 1
    while step < size:
        pad = jnp.full((1, step), neutral, row.dtype)
        row = combine(row, jnp.concatenate([pad, row[:, : size - step]], axis=1))
        step *= 2
    return row


def project_kernel(
    info, bias, x_ref, own_ref, other_ref, q_ref, kt_ref, v_ref, rows_ref, sent_ref, weight, gate, pre
):
    block = pl.program_id(0)

    @pl.when(block == 0)
    def _():
        core = info[0]
        for part in range(4):
            for z in range(NZ):
                columns = pl.ds(part * 128, 128)
                weight[z, core, :, columns] = own_ref[part, z, :HALF, :]
                weight[z, 1 - core, :, columns] = other_ref[part, z, :HALF, :]
        mine = jnp.sum(own_ref[0, :, HALF:, :].astype(jnp.float32), axis=1)
        theirs = jnp.sum(other_ref[0, :, HALF:, :].astype(jnp.float32), axis=1)
        first = jnp.where(core == 0, mine, theirs)
        second = jnp.where(core == 0, theirs, mine)
        inputs = jnp.concatenate([first[:, :HALF], second[:, :HALF]], axis=1)
        forgets = jnp.concatenate([first[:, HALF:], second[:, HALF:]], axis=1)
        gate[...] = jnp.zeros_like(gate)
        for z in range(NZ):
            columns = pl.ds(z * 128, 128)
            gate[0:1, columns] = inputs[z : z + 1]
            gate[1:2, columns] = forgets[z : z + 1]

    tokens = x_ref[0]
    projected = dot(tokens, weight[...].reshape(D, 2 * DK + DV))
    here = pl.ds(pl.multiple_of(block * TOK, TOK), TOK)
    q_ref[here, :] = projected[:, :DK].astype(jnp.bfloat16)
    kt_ref[:, here] = projected[:, DK : 2 * DK].T.astype(jnp.bfloat16)
    v_ref[here, :] = projected[:, 2 * DK :].astype(jnp.bfloat16)
    pre[:, here] = dot(gate[...].astype(jnp.bfloat16), tokens, ((1,), (1,)))

    @pl.when(block == NY - 1)
    def _():
        accepted = info[1]
        positions = info[2] * QUAD + lax.broadcasted_iota(jnp.int32, (1, QUAD), 1)
        live = positions < accepted
        forget_pre = pre[1:2, :] + bias[0]
        log_sigmoid = jnp.minimum(forget_pre, 0.0) - jnp.log1p(jnp.exp(-jnp.abs(forget_pre)))
        log_forget = jnp.where(live, log_sigmoid, 0.0)
        log_input = jnp.where(live, pre[0:1, :], lowest)
        decay_sum = scan_lanes(log_forget, jnp.add, 0.0)
        relative = log_input - decay_sum
        running_top = scan_lanes(relative, jnp.maximum, lowest)
        total = decay_sum[:, QUAD - 1 :]
        last_top = running_top[:, QUAD - 1 :]
        rows_ref[...] = jnp.concatenate(
            [relative, running_top, jnp.zeros((6, QUAD), jnp.float32)], axis=0
        )
        scaling = jnp.where(live, jnp.exp(relative - last_top), 0.0)
        weighted = (kt_ref[...].astype(jnp.float32) * scaling).astype(jnp.bfloat16)
        lane = lax.broadcasted_iota(jnp.int32, (QUAD, 128), 1)
        ones = jnp.where(lane == 0, 1.0, 0.0).astype(jnp.bfloat16)
        memory = dot(weighted, v_ref[...])
        normal = dot(weighted, ones)
        lane = lax.broadcasted_iota(jnp.int32, (DK, 128), 1)
        logs = normal
        for at, value in enumerate((*split3(total), *split3(total + last_top))):
            logs = jnp.where(lane == at + 1, value, logs)
        for to in range(NX):
            sent_ref[to, :, :DV] = memory.astype(jnp.bfloat16)
            sent_ref[to, :, DV:] = logs.astype(jnp.bfloat16)


def cell_kernel(info, q_ref, kt_ref, v_ref, rows_ref, states_ref, out_ref, carried, top_in):
    block = pl.program_id(0)

    @pl.when(block == 0)
    def _():
        place = info[2]
        state = jnp.zeros((DK, EXT), jnp.float32)
        top = jnp.full((1, 1), lowest, jnp.float32)
        for source in range(NX - 1):
            entry = states_ref[source].astype(jnp.float32)
            logs = entry[0:1, DV:]
            total = logs[:, 1:2] + (logs[:, 2:3] + logs[:, 3:4])
            top_part = logs[:, 4:5] + (logs[:, 5:6] + logs[:, 6:7])
            top_new = jnp.maximum(total + top, top_part)
            joined = jnp.exp(total + top - top_new) * state + jnp.exp(top_part - top_new) * entry
            state = jnp.where(source < place, joined, state)
            top = jnp.where(source < place, top_new, top)
        carried[...] = state.astype(jnp.bfloat16)
        top_in[...] = jnp.broadcast_to(top, (8, 128))

    scale = DK**-0.5
    carry_top = top_in[0:1, 0:1]
    for own in range(NY):

        @pl.when(block == own)
        def _():
            here = pl.ds(own * TOK, TOK)
            extent = (own + 1) * TOK
            columns = rows_ref[:, here].T
            top = jnp.maximum(columns[:, 1:2], carry_top)
            queries = q_ref[here, :]
            scores = dot(queries, kt_ref[:, :extent]) * scale
            relative = rows_ref[0:1, :extent] - top
            row = own * TOK + lax.broadcasted_iota(jnp.int32, (TOK, extent), 0)
            column = lax.broadcasted_iota(jnp.int32, (TOK, extent), 1)
            products = jnp.exp(jnp.where(row >= column, relative, lowest)) * scores
            carry = dot(queries, carried[...]) * (jnp.exp(carry_top - top) * scale)
            denominator = jnp.sum(products, axis=1, keepdims=True) + carry[:, DV : DV + 1]
            numerator = dot(products.astype(jnp.bfloat16), v_ref[:extent, :]) + carry[:, :DV]
            result = numerator / jnp.maximum(jnp.abs(denominator), 1.0)
            position = info[2] * QUAD + own * TOK + lax.broadcasted_iota(jnp.int32, (TOK, 1), 0)
            out_ref[0] = jnp.where(position < info[1], result, 0.0).astype(jnp.bfloat16)


SMEM = pl.BlockSpec(memory_space=pltpu.SMEM)


def whole(*shape):
    return pl.BlockSpec(shape, lambda block: (0,) * len(shape))


def project(info, bias, quad, own, other, **options):
    return pl.pallas_call(
        project_kernel,
        grid=(NY,),
        out_shape=(
            jax.ShapeDtypeStruct((QUAD, DK), jnp.bfloat16),
            jax.ShapeDtypeStruct((DK, QUAD), jnp.bfloat16),
            jax.ShapeDtypeStruct((QUAD, DV), jnp.bfloat16),
            jax.ShapeDtypeStruct((8, QUAD), jnp.float32),
            jax.ShapeDtypeStruct((NX, DK, EXT), jnp.bfloat16),
        ),
        in_specs=[
            SMEM,
            SMEM,
            pl.BlockSpec((1, TOK, D), lambda block: (block, 0, 0)),
            whole(4, NZ, PIECE, 128),
            whole(4, NZ, PIECE, 128),
        ],
        out_specs=(
            whole(QUAD, DK),
            whole(DK, QUAD),
            whole(QUAD, DV),
            whole(8, QUAD),
            whole(NX, DK, EXT),
        ),
        scratch_shapes=[
            pltpu.VMEM((NZ, NC, HALF, 2 * DK + DV), jnp.bfloat16),
            pltpu.VMEM((8, D), jnp.float32),
            pltpu.VMEM((8, QUAD), jnp.float32),
        ],
        compiler_params=pltpu.CompilerParams(vmem_limit_bytes=40 * 1024 * 1024),
        name="project",
        **options,
    )(info, bias, quad, own, other)


def cell(info, q, kt, v, rows, states, **options):
    return pl.pallas_call(
        cell_kernel,
        grid=(NY,),
        out_shape=jax.ShapeDtypeStruct((NY, TOK, DV), jnp.bfloat16),
        in_specs=[
            SMEM,
            whole(QUAD, DK),
            whole(DK, QUAD),
            whole(QUAD, DV),
            whole(8, QUAD),
            whole(NX, DK, EXT),
        ],
        out_specs=pl.BlockSpec((1, TOK, DV), lambda block: (block, 0, 0)),
        scratch_shapes=[pltpu.VMEM((DK, EXT), jnp.bfloat16), pltpu.VMEM((8, 128), jnp.float32)],
        compiler_params=pltpu.CompilerParams(vmem_limit_bytes=40 * 1024 * 1024),
        name="cell",
        **options,
    )(info, q, kt, v, rows, states)


def weight_piece(proj_weight, gate_weight, x, y):
    quarter = jnp.stack([y, H + y, 2 * H + 2 * y, 2 * H + 2 * y + 1])[x]
    columns = lax.dynamic_slice(proj_weight, (0, quarter * 128), (HALF, 128))
    pair = [lax.dynamic_slice(gate_weight, (0, at), (HALF, 1)) for at in (y, H + y)]
    row = jnp.concatenate(pair, axis=0).reshape(1, 2 * HALF)
    return jnp.concatenate([columns, row, jnp.zeros((7, 128), row.dtype)], axis=0)


def per_device(activations, proj_weight, gate_weight, forget_bias, accepted):
    x, y, core = (lax.axis_index(a) for a in ("x", "y", "c"))
    quad = lax.all_gather(activations, "y", axis=0, tiled=True)
    piece = weight_piece(proj_weight, gate_weight, x, y)
    rows = lax.all_to_all(jnp.tile(piece, (NZ, 1)), "z", 0, 0, tiled=True)
    own = lax.all_to_all(jnp.tile(rows, (NX, 1)), "x", 0, 0, tiled=True)
    other = lax.ppermute(own, "c", [(0, 1), (1, 0)])
    shape = (4, NZ, PIECE, 128)
    info = jnp.stack([core, accepted[0], x]).astype(jnp.int32)
    bias = lax.dynamic_slice(forget_bias, (y,), (1,))
    q, kt, v, gates, sent = project(info, bias, quad, own.reshape(shape), other.reshape(shape))
    states = lax.all_to_all(sent, "x", 0, 0, tiled=True)
    out = cell(info, q, kt, v, gates, states)
    heads = lax.all_to_all(out, "y", 0, 0, tiled=True)
    return heads.transpose(1, 0, 2).reshape(1, TOK, H * DV)


def solution(mesh):
    axes = Mesh(mesh.devices.reshape(NX, NY, NZ, NC), ("x", "y", "z", "c"))
    tokens = P(("z", "c"), ("x", "y"), None)
    weights = P(("z", "c"), None)
    return jax.shard_map(
        per_device,
        mesh=axes,
        in_specs=(tokens, weights, weights, P(), P(("z", "c"))),
        out_specs=tokens,
        check_vma=False,
    )
```

time: 217 us -> 114 us (0.53)
  the two profiles are of different devices: /device:TPU:30 before, /device:TPU:32 now
where the time goes in v1:
time: 114 us
  blocking collectives  77.3 us (68%)
  between operations  14.8 us (13%)
  Pallas kernels  10.4 us (9%)
  local copies, waits for them, and re-layouts  5.7 us (5%)
  waiting for transfers between devices  3.39 us (3%)
  starting transfers between devices  1.91 us (2%)
    all_to_all x1, blocking collectives, per_device(): rows = lax.all_to_all(jnp.tile(piece, (NZ, 1)), 'z', 0, 0, tiled=True)  33.8 us
    all_to_all x1, blocking collectives, per_device(): own = lax.all_to_all(jnp.tile(rows, (NX, 1)), 'x', 0, 0, tiled=True)  20 us
    all_to_all x1, blocking collectives, per_device(): states = lax.all_to_all(sent, 'x', 0, 0, tiled=True)  12.1 us
    all_to_all x1, blocking collectives, per_device(): heads = lax.all_to_all(out, 'y', 0, 0, tiled=True)  11.4 us
    pallas_call x1, Pallas kernels, project(): pl.pallas_call(project_kernel, grid=(NY,), out_shape=(jax.ShapeDtypeStruc...  6.69 us
    pallas_call x1, Pallas kernels, cell(): pl.pallas_call(cell_kernel, grid=(NY,), out_shape=jax.ShapeDtypeStruct((N...  3.68 us
  transfers between devices with their start and end apart: 2, of which 2 were waited for; matrix products, arithmetic and copies ran while one was open for 2% of the time, Pallas kernels for 0%

profile of v1, /device:TPU:32, one launch (start us, length us, event | category | flops | bytes accessed | tf_op | source)
XLA Modules:
  0.0 113.7 jit_solution(4794440363089858737)
XLA Ops:
  6.5 0.0 copy-start
  6.5 0.0 all-gather.2.cloned.1.call-start
  6.5 0.7 all-gather.2.cloned.1.call-update
  7.3 0.1 pad_add_fusion.1
  7.3 0.7 dynamic_slice.16
  8.7 0.1 pad.2.clone
  8.8 0.8 constant_dynamic-slice_fusion.1
  9.5 0.1 maximum_bitcast_fusion
  9.6 0.0 copy-done
  9.6 0.1 maximum_maximum_fusion
  9.7 33.8 %all_to_all.25 = bf16[16,72,128]{2,1,0:T(8,128)(2,1)S(1)} all-to-all(bf16[16,72,128]{2,1,0:T(8,128)(2,1)S(1)} %tile.6), channel_id=1, replica_groups=mesh['x'=4,'y'=4,'z'=16,'c'=2] {'z'}, dimensions={0} | all-to-all | bytes 589824 | tf_op jit(solution)/shard_map/all_to_all | solution.py:229
  43.5 0.2 tile.8
  43.7 0.0 copy-start.2
  43.7 20.0 %all_to_all.26 = bf16[4,1152,128]{2,1,0:T(8,128)(2,1)S(1)} all-to-all(bf16[4,1152,128]{2,1,0:T(8,128)(2,1)S(1)} %tile.8), channel_id=1, replica_groups=mesh['x'=4,'y'=4,'z'=16,'c'=2] {'x'}, dimensions={0} | all-to-all | bytes 2359296 | tf_op jit(solution)/shard_map/all_to_all | solution.py:230
  63.6 1.9 %collective-permute-start = (bf16[4608,128]{1,0:T(8,128)(2,1)S(1)}, bf16[4608,128]{1,0:T(8,128)(2,1)S(1)}, u32[]{:S(2)}, u32[]{:S(2)}) collective-permute-start(bf16[4608,128]{1,0:T(8,128)(2,1)S(1)} %bitcast.15), channel_id=1, source_target_pairs={{0,1},{1,0},{2,3},{3,2},{4,5},{5,4},{6,7},{7,6},{8,9},{9,8},{10,11... | collective-permute-start | bytes 3538952 | tf_op jit(solution)/shard_map/ppermute | solution.py:231
  66.2 0.0 copy-done.2
  66.2 0.6 dynamic_slice.15.bias
  66.8 0.1 pad_add_fusion.info
  66.9 1.5 %collective-permute-done = bf16[4608,128]{1,0:T(8,128)(2,1)S(1)} collective-permute-done((bf16[4608,128]{1,0:T(8,128)(2,1)S(1)}, bf16[4608,128]{1,0:T(8,128)(2,1)S(1)}, u32[]{:S(2)}, u32[]{:S(2)}) %collective-permute-start) | collective-permute-done | bytes 1179680 | tf_op jit(solution)/shard_map/ppermute | solution.py:231
  68.4 1.2 %all-gather.2.cloned.1.call-done.x_ref = bf16[4,256,2048]{2,1,0:T(8,128)(2,1)} async-done(((bf16[1,256,2048]{2,1,0:T(8,128)(2,1)}), bf16[4,256,2048]{2,1,0:T(8,128)(2,1)}) %all-gather.2.cloned.1.call-update) | async-done | bytes 4194320 | tf_op jit(solution)/shard_map/all_gather | solution.py:227
  69.6 0.0 copy-start.1
  69.6 2.2 %copy-done.1 = bf16[4,256,2048]{2,1,0:T(8,128)(2,1)S(1)} copy-done((bf16[4,256,2048]{2,1,0:T(8,128)(2,1)S(1)}, bf16[4,256,2048]{2,1,0:T(8,128)(2,1)}, u32[]{:S(2)}) %copy-start.1) | copy-done | bytes 4194328
  71.8 6.7 %project.1 = (bf16[1024,128]{1,0:T(8,128)(2,1)S(1)}, bf16[128,1024]{1,0:T(8,128)(2,1)S(1)}, bf16[1024,256]{1,0:T(8,128)(2,1)S(1)}, f32[8,1024]{1,0:T(8,128)S(1)}, bf16[4,128,384]{2,1,0:T(8,128)(2,1)S(1)}) custom-call(s32[3]{0:T(128)S(1)} %pad_add_fusion.info, f32[1]{0:T(128)} %dynamic_slice.15.bias, bf16[4,256,2048]{2,1,0:T(8,128)(2,1)S(1)} %copy-done.1, ...), custom_call_target="tpu_custom_call" | custom-call | tf_op jit(solution)/shard_map/project/pallas_call | solution.py:161
  78.5 12.1 %all_to_all.27.states_ref = bf16[4,128,384]{2,1,0:T(8,128)(2,1)S(1)} all-to-all(bf16[4,128,384]{2,1,0:T(8,128)(2,1)S(1)} %get-tuple-element.14), channel_id=1, replica_groups=mesh['x'=4,'y'=4,'z'=16,'c'=2] {'x'}, dimensions={0} | all-to-all | bytes 786432 | tf_op jit(solution)/shard_map/all_to_all | solution.py:236
  90.6 3.7 %cell.1 = bf16[4,256,256]{2,1,0:T(8,128)(2,1)S(1)} custom-call(s32[3]{0:T(128)S(1)} %pad_add_fusion.info, bf16[1024,128]{1,0:T(8,128)(2,1)S(1)} %get-tuple-element.10.q_ref, bf16[128,1024]{1,0:T(8,128)(2,1)S(1)} %get-tuple-element.11.kt_ref, bf16[1024,256]{1,0:T(8,128)(2,1)S(1)} %get-tuple-element.12.v_ref, f32[8,1024]{1,0:T(8,128)S(1)} %get-tuple-element.13.rows_ref, ...), custom_call_target="tpu_custom_call" | custom-call | tf_op jit(solution)/shard_map/cell/pallas_call | solution.py:197
  94.3 11.4 %all_to_all.28 = bf16[4,256,256]{2,1,0:T(8,128)(2,1)S(1)} all-to-all(bf16[4,256,256]{2,1,0:T(8,128)(2,1)S(1)} %cell.1), channel_id=1, replica_groups=mesh['x'=4,'y'=4,'z'=16,'c'=2] {'y'}, dimensions={0} | all-to-all | bytes 1048576 | tf_op jit(solution)/shard_map/all_to_all | solution.py:238
  105.7 0.2 copy.8
  105.9 1.0 copy.9
  (3 shorter events, 0.1 us)
Async XLA Ops:
  6.5 3.1 %copy-start = (bf16[64,2048]{1,0:T(8,128)(2,1)S(1)}, bf16[64,2048]{1,0:T(8,128)(2,1)}, u32[]{:S(2)}) copy-start(bf16[64,2048]{1,0:T(8,128)(2,1)} %param.6) | copy-start | bytes 786436
  6.5 63.0 %all-gather.2.cloned.1.call-start = ((), (), s32[]{:S(2)}) async-start(), calls=%async_computation.4 | async-start | bytes 5242880 | tf_op jit(solution)/shard_map/all_gather | solution.py:227
  43.7 22.5 %copy-start.2 = (f32[4]{0:T(128)S(1)}, f32[4]{0:T(128)}, u32[]{:S(2)}) copy-start(f32[4]{0:T(128)} %param.8) | copy-start | bytes 52
  63.6 4.7 %collective-permute-start = (bf16[4608,128]{1,0:T(8,128)(2,1)S(1)}, bf16[4608,128]{1,0:T(8,128)(2,1)S(1)}, u32[]{:S(2)}, u32[]{:S(2)}) collective-permute-start(bf16[4608,128]{1,0:T(8,128)(2,1)S(1)} %bitcast.15), channel_id=1, source_target_pairs={{0,1},{1,0},{2,3},{3,2},{4,5},{5,4},{6,7},{7,6},{8,9},{9,8},{10,11... | collective-permute-start | bytes 3538952 | tf_op jit(solution)/shard_map/ppermute | solution.py:231
  69.6 2.2 %copy-start.1 = (bf16[4,256,2048]{2,1,0:T(8,128)(2,1)S(1)}, bf16[4,256,2048]{2,1,0:T(8,128)(2,1)}, u32[]{:S(2)}) copy-start(bf16[4,256,2048]{2,1,0:T(8,128)(2,1)} %all-gather.2.cloned.1.call-done.x_ref) | copy-start | bytes 12582916
Sparse Core Ops, SparseCore 0:
  9.5 60.0 all-gather.1

commit v2 on v1

v2 whole, which is shorter than its diff:
```python
import functools

import jax
import jax.numpy as jnp
from jax import lax
from jax.experimental import pallas as pl
from jax.experimental.pallas import tpu as pltpu
from jax.sharding import Mesh
from jax.sharding import PartitionSpec as P

D = 2048
H = 4
DK = 128
DV = 256
TOK = 256
NX, NY, NZ, NC = 4, 4, 16, 2
QUAD = NY * TOK
HALF = D // (NZ * NC)
PIECE = HALF + 8
EXT = DV + 128
lowest = -1e30


def dot(a, b, contract=((1,), (0,))):
    return lax.dot_general(a, b, (contract, ((), ())), preferred_element_type=jnp.float32)


def split3(value):
    high = value.astype(jnp.bfloat16).astype(jnp.float32)
    rest = value - high
    middle = rest.astype(jnp.bfloat16).astype(jnp.float32)
    return high, middle, rest - middle


def scan_row(row, combine, neutral):
    lane = lax.broadcasted_iota(jnp.int32, (8, 128), 1)
    sub = lax.broadcasted_iota(jnp.int32, (8, 128), 0)
    chunk = jnp.concatenate([row[:, at * 128 : at * 128 + 128] for at in range(QUAD // 128)], axis=0)
    for step in (1, 2, 4, 8, 16, 32, 64):
        chunk = combine(chunk, jnp.where(lane >= step, pltpu.roll(chunk, step, 1), neutral))
    before = jnp.broadcast_to(chunk[:, 127:], (8, 128))
    before = jnp.where(sub >= 1, pltpu.roll(before, 1, 0), neutral)
    for step in (1, 2, 4):
        before = combine(before, jnp.where(sub >= step, pltpu.roll(before, step, 0), neutral))
    chunk = combine(chunk, before)
    return jnp.concatenate([chunk[at : at + 1, :] for at in range(QUAD // 128)], axis=1)


def assemble_kernel(info, own_ref, other_ref, weight_ref, gate_ref):
    core = info[0]
    for part in range(4):
        for z in range(NZ):
            columns = pl.ds(part * 128, 128)
            weight_ref[z, core, :, columns] = own_ref[part, z, :HALF, :]
            weight_ref[z, 1 - core, :, columns] = other_ref[part, z, :HALF, :]
    mine = jnp.sum(own_ref[0, :, HALF:, :].astype(jnp.float32), axis=1)
    theirs = jnp.sum(other_ref[0, :, HALF:, :].astype(jnp.float32), axis=1)
    first = jnp.where(core == 0, mine, theirs)
    second = jnp.where(core == 0, theirs, mine)
    inputs = jnp.concatenate([first[:, :HALF], second[:, :HALF]], axis=1)
    forgets = jnp.concatenate([first[:, HALF:], second[:, HALF:]], axis=1)
    gate_ref[...] = jnp.zeros_like(gate_ref)
    for z in range(NZ):
        columns = pl.ds(z * 128, 128)
        gate_ref[0:1, columns] = inputs[z : z + 1]
        gate_ref[1:2, columns] = forgets[z : z + 1]


def project_kernel(
    info, bias, x_hbm, weight_ref, gate_ref, q_ref, kt_ref, v_ref, rows_ref, sent_ref, tokens, arrived
):
    copies = [
        pltpu.make_async_copy(x_hbm.at[block], tokens.at[block], arrived.at[block])
        for block in range(NY)
    ]
    for copy in copies:
        copy.start()
    weight = weight_ref[...].reshape(D, 2 * DK + DV)
    gate = gate_ref[...].astype(jnp.bfloat16)
    pre = []
    for block in range(NY):
        copies[block].wait()
        here = pl.ds(block * TOK, TOK)
        pre.append(dot(gate, tokens[block], ((1,), (1,))))
        projected = dot(tokens[block], weight)
        q_ref[here, :] = projected[:, :DK].astype(jnp.bfloat16)
        kt_ref[:, here] = projected[:, DK : 2 * DK].T.astype(jnp.bfloat16)
        v_ref[here, :] = projected[:, 2 * DK :].astype(jnp.bfloat16)
    pre = jnp.concatenate(pre, axis=1)

    accepted = info[1]
    positions = info[2] * QUAD + lax.broadcasted_iota(jnp.int32, (1, QUAD), 1)
    live = positions < accepted
    forget_pre = pre[1:2, :] + bias[0]
    log_sigmoid = jnp.minimum(forget_pre, 0.0) - jnp.log1p(jnp.exp(-jnp.abs(forget_pre)))
    log_forget = jnp.where(live, log_sigmoid, 0.0)
    log_input = jnp.where(live, pre[0:1, :], lowest)
    decay_sum = scan_row(log_forget, jnp.add, 0.0)
    relative = log_input - decay_sum
    running_top = scan_row(relative, jnp.maximum, 2 * lowest)
    total = decay_sum[:, QUAD - 1 :]
    last_top = running_top[:, QUAD - 1 :]
    rows_ref[...] = jnp.concatenate(
        [relative, running_top, jnp.zeros((6, QUAD), jnp.float32)], axis=0
    )
    scaling = jnp.where(live, jnp.exp(relative - last_top), 0.0)
    weighted = kt_ref[...].astype(jnp.float32) * scaling
    normal = jnp.sum(weighted, axis=1, keepdims=True)
    memory = dot(weighted.astype(jnp.bfloat16), v_ref[...])
    lane = lax.broadcasted_iota(jnp.int32, (DK, 128), 1)
    logs = jnp.where(lane == 0, normal, 0.0)
    for at, value in enumerate((*split3(total), *split3(total + last_top))):
        logs = jnp.where(lane == at + 1, value, logs)
    sent_ref[:, :DV] = memory.astype(jnp.bfloat16)
    sent_ref[:, DV:] = logs.astype(jnp.bfloat16)


def cell_kernel(swaps, info, q_ref, kt_ref, v_ref, rows_ref, *refs):
    state_refs, out_refs = refs[: NX - 1], refs[NX - 1 :]
    place = info[2]
    state = jnp.zeros((DK, EXT), jnp.float32)
    carry_top = jnp.full((1, 1), lowest, jnp.float32)
    for distance in range(NX - 1, 0, -1):
        entry = state_refs[distance - 1][...].astype(jnp.float32)
        logs = entry[0:1, DV:]
        total = logs[:, 1:2] + (logs[:, 2:3] + logs[:, 3:4])
        top_part = logs[:, 4:5] + (logs[:, 5:6] + logs[:, 6:7])
        top_new = jnp.maximum(total + carry_top, top_part)
        joined = jnp.exp(total + carry_top - top_new) * state + jnp.exp(top_part - top_new) * entry
        state = jnp.where(place >= distance, joined, state)
        carry_top = jnp.where(place >= distance, top_new, carry_top)
    carried = state.astype(jnp.bfloat16)

    scale = DK**-0.5
    for swap, out_ref in zip(swaps, out_refs, strict=True):
        block = jnp.bitwise_xor(info[3], swap)
        for own in range(NY):

            @pl.when(block == own)
            def _(own=own, out_ref=out_ref):
                here = pl.ds(own * TOK, TOK)
                extent = (own + 1) * TOK
                columns = rows_ref[:, here].T
                top = jnp.maximum(columns[:, 1:2], carry_top)
                queries = q_ref[here, :]
                scores = dot(queries, kt_ref[:, :extent]) * scale
                relative = rows_ref[0:1, :extent] - top
                row = own * TOK + lax.broadcasted_iota(jnp.int32, (TOK, extent), 0)
                column = lax.broadcasted_iota(jnp.int32, (TOK, extent), 1)
                products = jnp.exp(jnp.where(row >= column, relative, lowest)) * scores
                carry = dot(queries, carried) * (jnp.exp(carry_top - top) * scale)
                denominator = jnp.sum(products, axis=1, keepdims=True) + carry[:, DV : DV + 1]
                numerator = dot(products.astype(jnp.bfloat16), v_ref[:extent, :]) + carry[:, :DV]
                result = numerator / jnp.maximum(jnp.abs(denominator), 1.0)
                at = place * QUAD + own * TOK + lax.broadcasted_iota(jnp.int32, (TOK, 1), 0)
                out_ref[...] = jnp.where(at < info[1], result, 0.0).astype(jnp.bfloat16)


def merge_kernel(info, *refs):
    for swap in range(H):
        head = jnp.bitwise_xor(info[3], swap)
        columns = pl.ds(pl.multiple_of(head * DV, DV), DV)
        refs[H][0, :, columns] = refs[swap][...]


SMEM = pl.BlockSpec(memory_space=pltpu.SMEM)
VMEM = pl.BlockSpec(memory_space=pltpu.VMEM)
PARAMS = pltpu.CompilerParams(vmem_limit_bytes=56 * 1024 * 1024)


def shaped(*shape, dtype=jnp.bfloat16):
    return jax.ShapeDtypeStruct(shape, dtype)


def assemble(info, own, other, **options):
    return pl.pallas_call(
        assemble_kernel,
        out_shape=(shaped(NZ, NC, HALF, 2 * DK + DV), shaped(8, D, dtype=jnp.float32)),
        in_specs=[SMEM, VMEM, VMEM],
        out_specs=(VMEM, VMEM),
        compiler_params=PARAMS,
        name="assemble",
        **options,
    )(info, own, other)


def project(info, bias, quad, weight, gate, **options):
    return pl.pallas_call(
        project_kernel,
        out_shape=(
            shaped(QUAD, DK),
            shaped(DK, QUAD),
            shaped(QUAD, DV),
            shaped(8, QUAD, dtype=jnp.float32),
            shaped(DK, EXT),
        ),
        in_specs=[SMEM, SMEM, pl.BlockSpec(memory_space=pl.ANY), VMEM, VMEM],
        out_specs=(VMEM,) * 5,
        scratch_shapes=[
            pltpu.VMEM((NY, TOK, D), jnp.bfloat16),
            pltpu.SemaphoreType.DMA((NY,)),
        ],
        compiler_params=PARAMS,
        name="project",
        **options,
    )(info, bias, quad, weight, gate)


def cell(swaps, info, q, kt, v, rows, states, **options):
    return pl.pallas_call(
        functools.partial(cell_kernel, swaps),
        out_shape=(shaped(TOK, DV),) * len(swaps),
        in_specs=[SMEM] + [VMEM] * (4 + len(states)),
        out_specs=(VMEM,) * len(swaps),
        compiler_params=PARAMS,
        name="cell",
        **options,
    )(info, q, kt, v, rows, *states)


def merge(info, heads, **options):
    return pl.pallas_call(
        merge_kernel,
        out_shape=shaped(1, TOK, H * DV),
        in_specs=[SMEM] + [VMEM] * H,
        out_specs=VMEM,
        compiler_params=PARAMS,
        name="merge",
        **options,
    )(info, *heads)


def weight_piece(proj_weight, gate_weight, x, y):
    quarter = jnp.stack([y, H + y, 2 * H + 2 * y, 2 * H + 2 * y + 1])[x]
    columns = lax.dynamic_slice(proj_weight, (0, quarter * 128), (HALF, 128))
    pair = [lax.dynamic_slice(gate_weight, (0, at), (HALF, 1)) for at in (y, H + y)]
    row = jnp.concatenate(pair, axis=0).reshape(1, 2 * HALF)
    return jnp.concatenate([columns, row, jnp.zeros((7, 128), row.dtype)], axis=0)


def per_device(activations, proj_weight, gate_weight, forget_bias, accepted):
    x, y, core = (lax.axis_index(a) for a in ("x", "y", "c"))
    quad = lax.all_gather(activations, "y", axis=0, tiled=True)
    piece = weight_piece(proj_weight, gate_weight, x, y)
    rows = lax.all_to_all(jnp.tile(piece, (NZ, 1)), "z", 0, 0, tiled=True)
    own = lax.all_to_all(jnp.tile(rows, (NX, 1)), "x", 0, 0, tiled=True)
    other = lax.ppermute(own, "c", [(0, 1), (1, 0)])
    shape = (4, NZ, PIECE, 128)
    info = jnp.stack([core, accepted[0], x, y]).astype(jnp.int32)
    bias = lax.dynamic_slice(forget_bias, (y,), (1,))
    weight, gate = assemble(info, own.reshape(shape), other.reshape(shape))
    q, kt, v, gates, sent = project(info, bias, quad, weight, gate)
    states = [
        lax.ppermute(sent, "x", [(i, i + distance) for i in range(NX - distance)])
        for distance in range(1, NX)
    ]
    parts = (info, q, kt, v, gates, states)
    theirs = cell((2, 1, 3), *parts)
    swapped = {
        swap: lax.ppermute(part, "y", [(i, i ^ swap) for i in range(NY)])
        for swap, part in zip((2, 1, 3), theirs, strict=True)
    }
    (mine,) = cell((0,), *parts)
    return merge(info, [mine, swapped[1], swapped[2], swapped[3]])


def solution(mesh):
    axes = Mesh(mesh.devices.reshape(NX, NY, NZ, NC), ("x", "y", "z", "c"))
    tokens = P(("z", "c"), ("x", "y"), None)
    weights = P(("z", "c"), None)
    return jax.shard_map(
        per_device,
        mesh=axes,
        in_specs=(tokens, weights, weights, P(), P(("z", "c"))),
        out_specs=tokens,
        check_vma=False,
    )
```

time: 114 us -> 125 us (1.096)
  the two profiles are of different devices: /device:TPU:32 before, /device:TPU:38 now
where the time goes in v2:
time: 125 us
  blocking collectives  52.1 us (42%)
  Pallas kernels  22.7 us (18%)
  starting transfers between devices  16.2 us (13%)
  between operations  14.9 us (12%)
  waiting for transfers between devices  13.2 us (11%)
  local copies, waits for them, and re-layouts  4.75 us (4%)
    all_to_all x1, blocking collectives, per_device(): rows = lax.all_to_all(jnp.tile(piece, (NZ, 1)), 'z', 0, 0, tiled=True)  33.8 us
    all_to_all x1, blocking collectives, per_device(): own = lax.all_to_all(jnp.tile(rows, (NX, 1)), 'x', 0, 0, tiled=True)  18.4 us
    ppermute x3, starting transfers between devices, per_device(): lax.ppermute(part, 'y', [(i, i ^ swap) for i in range(NY)])  10.4 us
    pallas_call x1, Pallas kernels, project(): pl.pallas_call(project_kernel, out_shape=(shaped(QUAD, DK), shaped(DK, QU...  9.98 us
    ppermute x3, waiting for transfers between devices, per_device(): lax.ppermute(sent, 'x', [(i, i + distance) for i in range(NX - distance)])  8.71 us
    pallas_call x2, Pallas kernels, cell(): pl.pallas_call(functools.partial(cell_kernel, swaps), out_shape=(shaped(T...  7.41 us
    ppermute x3, starting transfers between devices, per_device(): lax.ppermute(sent, 'x', [(i, i + distance) for i in range(NX - distance)])  3.88 us
    pallas_call x1, Pallas kernels, assemble(): pl.pallas_call(assemble_kernel, out_shape=(shaped(NZ, NC, HALF, 2 * DK +...  3.38 us
  transfers between devices with their start and end apart: 8, of which 5 were waited for; matrix products, arithmetic and copies ran while one was open for 3% of the time, Pallas kernels for 5%

profile of v2, /device:TPU:38, one launch (start us, length us, event | category | flops | bytes accessed | tf_op | source)
XLA Modules:
  0.0 124.8 jit_solution(5599369845592653435)
XLA Ops:
  6.5 0.0 copy-start
  6.5 0.0 all-gather.2.cloned.1.call-start
  6.5 0.7 all-gather.2.cloned.1.call-update
  7.3 0.1 pad_add_fusion.1
  7.3 0.7 dynamic_slice.16
  8.7 0.1 pad.2.clone
  8.8 0.8 constant_dynamic-slice_fusion.1
  9.5 0.1 maximum_bitcast_fusion
  9.6 0.0 copy-done
  9.6 0.1 maximum_maximum_fusion
  9.7 33.8 %all_to_all.15 = bf16[16,72,128]{2,1,0:T(8,128)(2,1)S(1)} all-to-all(bf16[16,72,128]{2,1,0:T(8,128)(2,1)S(1)} %tile.6), channel_id=1, replica_groups=mesh['x'=4,'y'=4,'z'=16,'c'=2] {'z'}, dimensions={0} | all-to-all | bytes 589824 | tf_op jit(solution)/shard_map/all_to_all | solution.py:245
  43.5 0.2 tile.8
  43.7 0.0 copy-start.9
  43.7 18.4 %all_to_all.16 = bf16[4,1152,128]{2,1,0:T(8,128)(2,1)S(1)} all-to-all(bf16[4,1152,128]{2,1,0:T(8,128)(2,1)S(1)} %tile.8), channel_id=1, replica_groups=mesh['x'=4,'y'=4,'z'=16,'c'=2] {'x'}, dimensions={0} | all-to-all | bytes 2359296 | tf_op jit(solution)/shard_map/all_to_all | solution.py:246
  62.0 0.0 copy-start.1
  62.0 1.9 %collective-permute-start = (bf16[4608,128]{1,0:T(8,128)(2,1)S(1)}, bf16[4608,128]{1,0:T(8,128)(2,1)S(1)}, u32[]{:S(2)}, u32[]{:S(2)}) collective-permute-start(bf16[4608,128]{1,0:T(8,128)(2,1)S(1)} %bitcast.13), channel_id=1, source_target_pairs={{0,1},{1,0},{2,3},{3,2},{4,5},{5,4},{6,7},{7,6},{8,9},{9,8},{10,11... | collective-permute-start | bytes 3538952 | tf_op jit(solution)/shard_map/ppermute | solution.py:247
  64.6 0.0 copy-done.9
  64.6 0.6 dynamic_slice.15.bias
  65.2 0.7 pad_add_fusion.info
  65.9 0.9 collective-permute-done
  66.8 0.0 copy-start.2
  66.8 0.0 copy-done.1
  66.8 1.1 copy-done.2
  67.9 3.4 %assemble.1 = (bf16[16,2,64,512]{3,2,1,0:T(8,128)(2,1)}, f32[8,2048]{1,0:T(8,128)}) custom-call(s32[4]{0:T(128)} %pad_add_fusion.info, bf16[4,16,72,128]{3,2,1,0:T(8,128)(2,1)} %bitcast.14, bf16[4,16,72,128]{3,2,1,0:T(8,128)(2,1)} %bitcast.15), custom_call_target="tpu_custom_call" | custom-call | tf_op jit(solution)/shard_map/assemble/pallas_call | solution.py:176
  71.3 0.0 all-gather.2.cloned.1.call-done.x_hbm
  71.3 10.0 %project.1 = (bf16[1024,128]{1,0:T(8,128)(2,1)}, bf16[128,1024]{1,0:T(8,128)(2,1)}, bf16[1024,256]{1,0:T(8,128)(2,1)}, f32[8,1024]{1,0:T(8,128)}, bf16[128,384]{1,0:T(8,128)(2,1)}) custom-call(s32[4]{0:T(128)} %pad_add_fusion.info, f32[1]{0:T(128)} %dynamic_slice.15.bias, bf16[4,256,2048]{2,1,0:T(8,128)(2,1)} %all-gather.2.cloned.1.call-done.x_hbm, ...), custom_call_target="tpu_custom_call" | custom-call | tf_op jit(solution)/shard_map/project/pallas_call | solution.py:188
  81.3 1.3 %collective-permute-start.1 = (bf16[128,384]{1,0:T(8,128)(2,1)}, bf16[128,384]{1,0:T(8,128)(2,1)S(1)}, u32[]{:S(2)}, u32[]{:S(2)}) collective-permute-start(bf16[128,384]{1,0:T(8,128)(2,1)} %get-tuple-element.21), channel_id=1, source_target_pairs={{0,128},{128,256},{256,384},{1,129},{129,257},{257,385},{2,130},{1... | collective-permute-start | bytes 294920 | tf_op jit(solution)/shard_map/ppermute | solution.py:254
  82.6 1.3 %collective-permute-start.2 = (bf16[128,384]{1,0:T(8,128)(2,1)}, bf16[128,384]{1,0:T(8,128)(2,1)S(1)}, u32[]{:S(2)}, u32[]{:S(2)}) collective-permute-start(bf16[128,384]{1,0:T(8,128)(2,1)} %get-tuple-element.21), channel_id=1, source_target_pairs={{0,256},{128,384},{1,257},{129,385},{2,258},{130,386},{3,259},{131... | collective-permute-start | bytes 294920 | tf_op jit(solution)/shard_map/ppermute | solution.py:254
  83.9 1.3 %collective-permute-start.3 = (bf16[128,384]{1,0:T(8,128)(2,1)}, bf16[128,384]{1,0:T(8,128)(2,1)S(1)}, u32[]{:S(2)}, u32[]{:S(2)}) collective-permute-start(bf16[128,384]{1,0:T(8,128)(2,1)} %get-tuple-element.21), channel_id=1, source_target_pairs={{0,384},{1,385},{2,386},{3,387},{4,388},{5,389},{6,390},{7,391},{8... | collective-permute-start | bytes 294920 | tf_op jit(solution)/shard_map/ppermute | solution.py:254
  85.2 3.0 %collective-permute-done.1.refs_0_ = bf16[128,384]{1,0:T(8,128)(2,1)S(1)} collective-permute-done((bf16[128,384]{1,0:T(8,128)(2,1)}, bf16[128,384]{1,0:T(8,128)(2,1)S(1)}, u32[]{:S(2)}, u32[]{:S(2)}) %collective-permute-start.1) | collective-permute-done | bytes 98336 | tf_op jit(solution)/shard_map/ppermute | solution.py:254
  88.2 0.0 copy-start.3
  88.2 2.8 %collective-permute-done.2.refs_1_ = bf16[128,384]{1,0:T(8,128)(2,1)S(1)} collective-permute-done((bf16[128,384]{1,0:T(8,128)(2,1)}, bf16[128,384]{1,0:T(8,128)(2,1)S(1)}, u32[]{:S(2)}, u32[]{:S(2)}) %collective-permute-start.2) | collective-permute-done | bytes 98336 | tf_op jit(solution)/shard_map/ppermute | solution.py:254
  91.0 0.0 copy-start.4
  91.0 2.9 %collective-permute-done.3.refs_2_ = bf16[128,384]{1,0:T(8,128)(2,1)S(1)} collective-permute-done((bf16[128,384]{1,0:T(8,128)(2,1)}, bf16[128,384]{1,0:T(8,128)(2,1)S(1)}, u32[]{:S(2)}, u32[]{:S(2)}) %collective-permute-start.3) | collective-permute-done | bytes 98336 | tf_op jit(solution)/shard_map/ppermute | solution.py:254
  93.9 0.0 copy-start.5
  93.9 0.0 copy-done.3
  93.9 0.0 copy-done.4
  93.9 0.6 copy-done.5
  94.5 4.5 %cell.3 = (bf16[256,256]{1,0:T(8,128)(2,1)}, bf16[256,256]{1,0:T(8,128)(2,1)}, bf16[256,256]{1,0:T(8,128)(2,1)}) custom-call(s32[4]{0:T(128)} %pad_add_fusion.info, bf16[1024,128]{1,0:T(8,128)(2,1)} %get-tuple-element.17.q_ref, bf16[128,1024]{1,0:T(8,128)(2,1)} %get-tuple-element.18.kt_ref, bf16[1024,256]{1,0:T(8,128)(2,1)} %get-tuple-element.19.v_ref, ...), custom_call_target="tpu_custom_call" | custom-call | tf_op jit(solution)/shard_map/cell/pallas_call | solution.py:210
  99.0 3.5 %collective-permute-start.4 = (bf16[256,256]{1,0:T(8,128)(2,1)}, bf16[256,256]{1,0:T(8,128)(2,1)S(1)}, u32[]{:S(2)}, u32[]{:S(2)}) collective-permute-start(bf16[256,256]{1,0:T(8,128)(2,1)} %get-tuple-element.22), channel_id=1, source_target_pairs={{0,32},{32,0},{64,96},{96,64},{1,33},{33,1},{65,97},{97,65},{2,34}... | collective-permute-start | bytes 393224 | tf_op jit(solution)/shard_map/ppermute | solution.py:260
  102.5 4.6 %collective-permute-start.5 = (bf16[256,256]{1,0:T(8,128)(2,1)}, bf16[256,256]{1,0:T(8,128)(2,1)S(1)}, u32[]{:S(2)}, u32[]{:S(2)}) collective-permute-start(bf16[256,256]{1,0:T(8,128)(2,1)} %get-tuple-element.23), channel_id=1, source_target_pairs={{0,64},{32,96},{64,0},{96,32},{1,65},{33,97},{65,1},{97,33},{2,66}... | collective-permute-start | bytes 393224 | tf_op jit(solution)/shard_map/ppermute | solution.py:260
  107.0 2.4 %collective-permute-start.6 = (bf16[256,256]{1,0:T(8,128)(2,1)}, bf16[256,256]{1,0:T(8,128)(2,1)S(1)}, u32[]{:S(2)}, u32[]{:S(2)}) collective-permute-start(bf16[256,256]{1,0:T(8,128)(2,1)} %get-tuple-element.24), channel_id=1, source_target_pairs={{0,96},{32,64},{64,32},{96,0},{1,97},{33,65},{65,33},{97,1},{2,98}... | collective-permute-start | bytes 393224 | tf_op jit(solution)/shard_map/ppermute | solution.py:260
  109.4 3.0 %cell.2.refs_0_ = bf16[256,256]{1,0:T(8,128)(2,1)} custom-call(s32[4]{0:T(128)} %pad_add_fusion.info, bf16[1024,128]{1,0:T(8,128)(2,1)} %get-tuple-element.17.q_ref, bf16[128,1024]{1,0:T(8,128)(2,1)} %get-tuple-element.18.kt_ref, bf16[1024,256]{1,0:T(8,128)(2,1)} %get-tuple-element.19.v_ref, f32[8,1024]{1,0:T(8,128)} %get-tuple-element.20.rows_ref, ...), custom_call_target="tpu_custom_call" | custom-call | tf_op jit(solution)/shard_map/cell/pallas_call | solution.py:210
  112.4 0.0 collective-permute-done.4.refs_1_
  112.4 0.0 copy-start.6
  112.4 0.0 collective-permute-done.5.refs_2_
  112.4 0.0 copy-start.7
  112.4 2.9 %collective-permute-done.6.refs_3_ = bf16[256,256]{1,0:T(8,128)(2,1)S(1)} collective-permute-done((bf16[256,256]{1,0:T(8,128)(2,1)}, bf16[256,256]{1,0:T(8,128)(2,1)S(1)}, u32[]{:S(2)}, u32[]{:S(2)}) %collective-permute-start.6) | collective-permute-done | bytes 131104 | tf_op jit(solution)/shard_map/ppermute | solution.py:260
  115.3 0.0 copy-done.6
  115.3 0.0 copy-done.7
  115.3 0.0 copy-start.8
  115.3 0.7 copy-done.8
  116.0 2.0 %merge.1 = bf16[1,256,1024]{2,1,0:T(8,128)(2,1)} custom-call(s32[4]{0:T(128)} %pad_add_fusion.info, bf16[256,256]{1,0:T(8,128)(2,1)} %cell.2.refs_0_, bf16[256,256]{1,0:T(8,128)(2,1)} %copy-done.6, bf16[256,256]{1,0:T(8,128)(2,1)} %copy-done.7, bf16[256,256]{1,0:T(8,128)(2,1)} %copy-done.8), custom_call_target="tpu_custom_call" | custom-call | tf_op jit(solution)/shard_map/merge/pallas_call | solution.py:222
  (3 shorter events, 0.1 us)
Async XLA Ops:
  6.5 3.1 %copy-start = (bf16[64,2048]{1,0:T(8,128)(2,1)S(1)}, bf16[64,2048]{1,0:T(8,128)(2,1)}, u32[]{:S(2)}) copy-start(bf16[64,2048]{1,0:T(8,128)(2,1)} %param.6) | copy-start | bytes 786436
  6.5 64.8 %all-gather.2.cloned.1.call-start = ((), (), s32[]{:S(2)}) async-start(), calls=%async_computation.2 | async-start | bytes 5242880 | tf_op jit(solution)/shard_map/all_gather | solution.py:243
  43.7 20.9 %copy-start.9 = (f32[4]{0:T(128)S(1)}, f32[4]{0:T(128)}, u32[]{:S(2)}) copy-start(f32[4]{0:T(128)} %param.8) | copy-start | bytes 52
  62.0 4.7 %copy-start.1 = (bf16[4,1152,128]{2,1,0:T(8,128)(2,1)}, bf16[4,1152,128]{2,1,0:T(8,128)(2,1)S(1)}, u32[]{:S(2)}) copy-start(bf16[4,1152,128]{2,1,0:T(8,128)(2,1)S(1)} %all_to_all.16) | copy-start | bytes 3538948
  62.0 4.7 %collective-permute-start = (bf16[4608,128]{1,0:T(8,128)(2,1)S(1)}, bf16[4608,128]{1,0:T(8,128)(2,1)S(1)}, u32[]{:S(2)}, u32[]{:S(2)}) collective-permute-start(bf16[4608,128]{1,0:T(8,128)(2,1)S(1)} %bitcast.13), channel_id=1, source_target_pairs={{0,1},{1,0},{2,3},{3,2},{4,5},{5,4},{6,7},{7,6},{8,9},{9,8},{10,11... | collective-permute-start | bytes 3538952 | tf_op jit(solution)/shard_map/ppermute | solution.py:247
  66.8 1.1 copy-start.2
  81.3 6.9 %collective-permute-start.1 = (bf16[128,384]{1,0:T(8,128)(2,1)}, bf16[128,384]{1,0:T(8,128)(2,1)S(1)}, u32[]{:S(2)}, u32[]{:S(2)}) collective-permute-start(bf16[128,384]{1,0:T(8,128)(2,1)} %get-tuple-element.21), channel_id=1, source_target_pairs={{0,128},{128,256},{256,384},{1,129},{129,257},{257,385},{2,130},{1... | collective-permute-start | bytes 294920 | tf_op jit(solution)/shard_map/ppermute | solution.py:254
  82.6 8.4 %collective-permute-start.2 = (bf16[128,384]{1,0:T(8,128)(2,1)}, bf16[128,384]{1,0:T(8,128)(2,1)S(1)}, u32[]{:S(2)}, u32[]{:S(2)}) collective-permute-start(bf16[128,384]{1,0:T(8,128)(2,1)} %get-tuple-element.21), channel_id=1, source_target_pairs={{0,256},{128,384},{1,257},{129,385},{2,258},{130,386},{3,259},{131... | collective-permute-start | bytes 294920 | tf_op jit(solution)/shard_map/ppermute | solution.py:254
  83.9 10.0 %collective-permute-start.3 = (bf16[128,384]{1,0:T(8,128)(2,1)}, bf16[128,384]{1,0:T(8,128)(2,1)S(1)}, u32[]{:S(2)}, u32[]{:S(2)}) collective-permute-start(bf16[128,384]{1,0:T(8,128)(2,1)} %get-tuple-element.21), channel_id=1, source_target_pairs={{0,384},{1,385},{2,386},{3,387},{4,388},{5,389},{6,390},{7,391},{8... | collective-permute-start | bytes 294920 | tf_op jit(solution)/shard_map/ppermute | solution.py:254
  88.2 5.7 %copy-start.3 = (bf16[128,384]{1,0:T(8,128)(2,1)}, bf16[128,384]{1,0:T(8,128)(2,1)S(1)}, u32[]{:S(2)}) copy-start(bf16[128,384]{1,0:T(8,128)(2,1)S(1)} %collective-permute-done.1.refs_0_) | copy-start | bytes 294916
  91.0 2.9 %copy-start.4 = (bf16[128,384]{1,0:T(8,128)(2,1)}, bf16[128,384]{1,0:T(8,128)(2,1)S(1)}, u32[]{:S(2)}) copy-start(bf16[128,384]{1,0:T(8,128)(2,1)S(1)} %collective-permute-done.2.refs_1_) | copy-start | bytes 294916
  93.9 0.6 copy-start.5
  99.0 13.4 %collective-permute-start.4 = (bf16[256,256]{1,0:T(8,128)(2,1)}, bf16[256,256]{1,0:T(8,128)(2,1)S(1)}, u32[]{:S(2)}, u32[]{:S(2)}) collective-permute-start(bf16[256,256]{1,0:T(8,128)(2,1)} %get-tuple-element.22), channel_id=1, source_target_pairs={{0,32},{32,0},{64,96},{96,64},{1,33},{33,1},{65,97},{97,65},{2,34}... | collective-permute-start | bytes 393224 | tf_op jit(solution)/shard_map/ppermute | solution.py:260
  102.5 9.9 %collective-permute-start.5 = (bf16[256,256]{1,0:T(8,128)(2,1)}, bf16[256,256]{1,0:T(8,128)(2,1)S(1)}, u32[]{:S(2)}, u32[]{:S(2)}) collective-permute-start(bf16[256,256]{1,0:T(8,128)(2,1)} %get-tuple-element.23), channel_id=1, source_target_pairs={{0,64},{32,96},{64,0},{96,32},{1,65},{33,97},{65,1},{97,33},{2,66}... | collective-permute-start | bytes 393224 | tf_op jit(solution)/shard_map/ppermute | solution.py:260
  107.0 8.3 %collective-permute-start.6 = (bf16[256,256]{1,0:T(8,128)(2,1)}, bf16[256,256]{1,0:T(8,128)(2,1)S(1)}, u32[]{:S(2)}, u32[]{:S(2)}) collective-permute-start(bf16[256,256]{1,0:T(8,128)(2,1)} %get-tuple-element.24), channel_id=1, source_target_pairs={{0,96},{32,64},{64,32},{96,0},{1,97},{33,65},{65,33},{97,1},{2,98}... | collective-permute-start | bytes 393224 | tf_op jit(solution)/shard_map/ppermute | solution.py:260
  112.4 3.0 %copy-start.6 = (bf16[256,256]{1,0:T(8,128)(2,1)}, bf16[256,256]{1,0:T(8,128)(2,1)S(1)}, u32[]{:S(2)}) copy-start(bf16[256,256]{1,0:T(8,128)(2,1)S(1)} %collective-permute-done.4.refs_1_) | copy-start | bytes 393220
  112.4 3.0 %copy-start.7 = (bf16[256,256]{1,0:T(8,128)(2,1)}, bf16[256,256]{1,0:T(8,128)(2,1)S(1)}, u32[]{:S(2)}) copy-start(bf16[256,256]{1,0:T(8,128)(2,1)S(1)} %collective-permute-done.5.refs_2_) | copy-start | bytes 393220
  115.3 0.7 copy-start.8
Sparse Core Ops, SparseCore 0:
  9.5 59.9 all-gather.1

commit v3 on v2

--- a/solution.py
+++ b/solution.py
@@ -1,5 +1,3 @@
-import functools
-
 import jax
 import jax.numpy as jnp
 from jax import lax
@@ -111,61 +109,57 @@
     logs = jnp.where(lane == 0, normal, 0.0)
     for at, value in enumerate((*split3(total), *split3(total + last_top))):
         logs = jnp.where(lane == at + 1, value, logs)
-    sent_ref[:, :DV] = memory.astype(jnp.bfloat16)
-    sent_ref[:, DV:] = logs.astype(jnp.bfloat16)
-
-
-def cell_kernel(swaps, info, q_ref, kt_ref, v_ref, rows_ref, *refs):
-    state_refs, out_refs = refs[: NX - 1], refs[NX - 1 :]
+    for to in range(NX):
+        sent_ref[to, :, :DV] = memory.astype(jnp.bfloat16)
+        sent_ref[to, :, DV:] = logs.astype(jnp.bfloat16)
+
+
+def cell_kernel(info, q_ref, kt_ref, v_ref, rows_ref, states_ref, out_ref):
     place = info[2]
     state = jnp.zeros((DK, EXT), jnp.float32)
     carry_top = jnp.full((1, 1), lowest, jnp.float32)
-    for distance in range(NX - 1, 0, -1):
-        entry = state_refs[distance - 1][...].astype(jnp.float32)
+    for source in range(NX - 1):
+        entry = states_ref[source].astype(jnp.float32)
         logs = entry[0:1, DV:]
         total = logs[:, 1:2] + (logs[:, 2:3] + logs[:, 3:4])
         top_part = logs[:, 4:5] + (logs[:, 5:6] + logs[:, 6:7])
         top_new = jnp.maximum(total + carry_top, top_part)
         joined = jnp.exp(total + carry_top - top_new) * state + jnp.exp(top_part - top_new) * entry
-        state = jnp.where(place >= distance, joined, state)
-        carry_top = jnp.where(place >= distance, top_new, carry_top)
+        state = jnp.where(source < place, joined, state)
+        carry_top = jnp.where(source < place, top_new, carry_top)
     carried = state.astype(jnp.bfloat16)
 
     scale = DK**-0.5
-    for swap, out_ref in zip(swaps, out_refs, strict=True):
-        block = jnp.bitwise_xor(info[3], swap)
-        for own in range(NY):
-
-            @pl.when(block == own)
-            def _(own=own, out_ref=out_ref):
-                here = pl.ds(own * TOK, TOK)
-                extent = (own + 1) * TOK
-                columns = rows_ref[:, here].T
-                top = jnp.maximum(columns[:, 1:2], carry_top)
-                queries = q_ref[here, :]
-                scores = dot(queries, kt_ref[:, :extent]) * scale
-                relative = rows_ref[0:1, :extent] - top
-                row = own * TOK + lax.broadcasted_iota(jnp.int32, (TOK, extent), 0)
-                column = lax.broadcasted_iota(jnp.int32, (TOK, extent), 1)
-                products = jnp.exp(jnp.where(row >= column, relative, lowest)) * scores
-                carry = dot(queries, carried) * (jnp.exp(carry_top - top) * scale)
-                denominator = jnp.sum(products, axis=1, keepdims=True) + carry[:, DV : DV + 1]
-                numerator = dot(products.astype(jnp.bfloat16), v_ref[:extent, :]) + carry[:, :DV]
-                result = numerator / jnp.maximum(jnp.abs(denominator), 1.0)
-                at = place * QUAD + own * TOK + lax.broadcasted_iota(jnp.int32, (TOK, 1), 0)
-                out_ref[...] = jnp.where(at < info[1], result, 0.0).astype(jnp.bfloat16)
-
-
-def merge_kernel(info, *refs):
-    for swap in range(H):
-        head = jnp.bitwise_xor(info[3], swap)
-        columns = pl.ds(pl.multiple_of(head * DV, DV), DV)
-        refs[H][0, :, columns] = refs[swap][...]
+    columns = rows_ref[...].T
+    for block in range(NY):
+        here = pl.ds(block * TOK, TOK)
+        extent = (block + 1) * TOK
+        top = jnp.maximum(columns[block * TOK : extent, 1:2], carry_top)
+        queries = q_ref[here, :]
+        scores = dot(queries, kt_ref[:, :extent]) * scale
+        relative = rows_ref[0:1, :extent] - top
+        row = block * TOK + lax.broadcasted_iota(jnp.int32, (TOK, extent), 0)
+        column = lax.broadcasted_iota(jnp.int32, (TOK, extent), 1)
+        products = jnp.exp(jnp.where(row >= column, relative, lowest)) * scores
+        carry = dot(queries, carried) * (jnp.exp(carry_top - top) * scale)
+        denominator = jnp.sum(products, axis=1, keepdims=True) + carry[:, DV : DV + 1]
+        numerator = dot(products.astype(jnp.bfloat16), v_ref[:extent, :]) + carry[:, :DV]
+        result = numerator / jnp.maximum(jnp.abs(denominator), 1.0)
+        at = place * QUAD + block * TOK + lax.broadcasted_iota(jnp.int32, (TOK, 1), 0)
+        out_ref[block] = jnp.where(at < info[1], result, 0.0).astype(jnp.bfloat16)
+
+
+def merge_kernel(heads_ref, out_ref):
+    for head in range(H):
+        out_ref[0, :, head * DV : (head + 1) * DV] = heads_ref[head]
 
 
 SMEM = pl.BlockSpec(memory_space=pltpu.SMEM)
 VMEM = pl.BlockSpec(memory_space=pltpu.VMEM)
-PARAMS = pltpu.CompilerParams(vmem_limit_bytes=56 * 1024 * 1024)
+
+
+def granted(mebibytes):
+    return pltpu.CompilerParams(vmem_limit_bytes=mebibytes * 1024 * 1024)
 
 
 def shaped(*shape, dtype=jnp.bfloat16):
@@ -178,7 +172,7 @@
         out_shape=(shaped(NZ, NC, HALF, 2 * DK + DV), shaped(8, D, dtype=jnp.float32)),
         in_specs=[SMEM, VMEM, VMEM],
         out_specs=(VMEM, VMEM),
-        compiler_params=PARAMS,
+        compiler_params=granted(16),
         name="assemble",
         **options,
     )(info, own, other)
@@ -192,42 +186,42 @@
             shaped(DK, QUAD),
             shaped(QUAD, DV),
             shaped(8, QUAD, dtype=jnp.float32),
-            shaped(DK, EXT),
+            shaped(NX, DK, EXT),
         ),
-        in_specs=[SMEM, SMEM, pl.BlockSpec(memory_space=pl.ANY), VMEM, VMEM],
+        in_specs=[SMEM, SMEM, pl.BlockSpec(memory_space=pltpu.HBM), VMEM, VMEM],
         out_specs=(VMEM,) * 5,
         scratch_shapes=[
             pltpu.VMEM((NY, TOK, D), jnp.bfloat16),
             pltpu.SemaphoreType.DMA((NY,)),
         ],
-        compiler_params=PARAMS,
+        compiler_params=granted(24),
         name="project",
         **options,
     )(info, bias, quad, weight, gate)
 
 
-def cell(swaps, info, q, kt, v, rows, states, **options):
-    return pl.pallas_call(
-        functools.partial(cell_kernel, swaps),
-        out_shape=(shaped(TOK, DV),) * len(swaps),
-        in_specs=[SMEM] + [VMEM] * (4 + len(states)),
-        out_specs=(VMEM,) * len(swaps),
-        compiler_params=PARAMS,
+def cell(info, q, kt, v, rows, states, **options):
+    return pl.pallas_call(
+        cell_kernel,
+        out_shape=shaped(NY, TOK, DV),
+        in_specs=[SMEM] + [VMEM] * 5,
+        out_specs=VMEM,
+        compiler_params=granted(16),
         name="cell",
         **options,
-    )(info, q, kt, v, rows, *states)
-
-
-def merge(info, heads, **options):
+    )(info, q, kt, v, rows, states)
+
+
+def merge(heads, **options):
     return pl.pallas_call(
         merge_kernel,
         out_shape=shaped(1, TOK, H * DV),
-        in_specs=[SMEM] + [VMEM] * H,
+        in_specs=[VMEM],
         out_specs=VMEM,
-        compiler_params=PARAMS,
+        compiler_params=granted(8),
         name="merge",
         **options,
-    )(info, *heads)
+    )(heads)
 
 
 def weight_piece(proj_weight, gate_weight, x, y):
@@ -246,22 +240,13 @@
     own = lax.all_to_all(jnp.tile(rows, (NX, 1)), "x", 0, 0, tiled=True)
     other = lax.ppermute(own, "c", [(0, 1), (1, 0)])
     shape = (4, NZ, PIECE, 128)
-    info = jnp.stack([core, accepted[0], x, y]).astype(jnp.int32)
+    info = jnp.stack([core, accepted[0], x]).astype(jnp.int32)
     bias = lax.dynamic_slice(forget_bias, (y,), (1,))
     weight, gate = assemble(info, own.reshape(shape), other.reshape(shape))
     q, kt, v, gates, sent = project(info, bias, quad, weight, gate)
-    states = [
-        lax.ppermute(sent, "x", [(i, i + distance) for i in range(NX - distance)])
-        for distance in range(1, NX)
-    ]
-    parts = (info, q, kt, v, gates, states)
-    theirs = cell((2, 1, 3), *parts)
-    swapped = {
-        swap: lax.ppermute(part, "y", [(i, i ^ swap) for i in range(NY)])
-        for swap, part in zip((2, 1, 3), theirs, strict=True)
-    }
-    (mine,) = cell((0,), *parts)
-    return merge(info, [mine, swapped[1], swapped[2], swapped[3]])
+    states = lax.all_to_all(sent, "x", 0, 0, tiled=True)
+    out = cell(info, q, kt, v, gates, states)
+    return merge(lax.all_to_all(out, "y", 0, 0, tiled=True))
 
 
 def solution(mesh):

time: 125 us -> 118 us (0.944)
  the two profiles are of different devices: /device:TPU:38 before, /device:TPU:32 now
where the time goes in v3:
time: 118 us; the launch traced here: 117 us
  blocking collectives  78 us (66%)
  between operations  14.7 us (12%)
  Pallas kernels  11.9 us (10%)
  local copies, waits for them, and re-layouts  8.23 us (7%)
  waiting for transfers between devices  2.15 us (2%)
  starting transfers between devices  1.91 us (2%)
    all_to_all x1, blocking collectives, per_device(): rows = lax.all_to_all(jnp.tile(piece, (NZ, 1)), 'z', 0, 0, tiled=True)  33.8 us
    all_to_all x1, blocking collectives, per_device(): own = lax.all_to_all(jnp.tile(rows, (NX, 1)), 'x', 0, 0, tiled=True)  20 us
    all_to_all x1, blocking collectives, per_device(): return merge(lax.all_to_all(out, 'y', 0, 0, tiled=True))  13.2 us
    all_to_all x1, blocking collectives, per_device(): states = lax.all_to_all(sent, 'x', 0, 0, tiled=True)  11 us
    pallas_call x1, Pallas kernels, project(): pl.pallas_call(project_kernel, out_shape=(shaped(QUAD, DK), shaped(DK, QU...  7.49 us
    unnamed x14, local copies, waits for them, and re-layouts  5.95 us
    pallas_call x1, Pallas kernels, cell(): pl.pallas_call(cell_kernel, out_shape=shaped(NY, TOK, DV), in_specs=[SMEM...  2.65 us
  transfers between devices with their start and end apart: 2, of which 1 were waited for; matrix products, arithmetic and copies ran while one was open for 2% of the time, Pallas kernels for 1%

profile of v3, /device:TPU:32, one launch (start us, length us, event | category | flops | bytes accessed | tf_op | source)
XLA Modules:
  0.0 117.2 jit_solution(15897625420603775783)
XLA Ops:
  6.5 0.0 copy-start
  6.5 0.0 all-gather.2.cloned.1.call-start
  6.5 0.7 all-gather.2.cloned.1.call-update
  7.3 0.1 pad_add_fusion.1
  7.3 0.6 dynamic_slice.16
  8.5 0.1 pad.2.clone
  8.6 0.8 constant_dynamic-slice_fusion.1
  9.4 0.1 maximum_bitcast_fusion
  9.5 0.0 copy-done
  9.5 0.1 maximum_maximum_fusion
  9.6 33.8 %all_to_all.25 = bf16[16,72,128]{2,1,0:T(8,128)(2,1)S(1)} all-to-all(bf16[16,72,128]{2,1,0:T(8,128)(2,1)S(1)} %tile.6), channel_id=1, replica_groups=mesh['x'=4,'y'=4,'z'=16,'c'=2] {'z'}, dimensions={0} | all-to-all | bytes 589824 | tf_op jit(solution)/shard_map/all_to_all | solution.py:239
  43.4 0.2 tile.8
  43.5 0.0 copy-start.6
  43.5 20.0 %all_to_all.26 = bf16[4,1152,128]{2,1,0:T(8,128)(2,1)S(1)} all-to-all(bf16[4,1152,128]{2,1,0:T(8,128)(2,1)S(1)} %tile.8), channel_id=1, replica_groups=mesh['x'=4,'y'=4,'z'=16,'c'=2] {'x'}, dimensions={0} | all-to-all | bytes 2359296 | tf_op jit(solution)/shard_map/all_to_all | solution.py:240
  63.5 1.9 %collective-permute-start = (bf16[4608,128]{1,0:T(8,128)(2,1)S(1)}, bf16[4608,128]{1,0:T(8,128)(2,1)S(1)}, u32[]{:S(2)}, u32[]{:S(2)}) collective-permute-start(bf16[4608,128]{1,0:T(8,128)(2,1)S(1)} %bitcast.13), channel_id=1, source_target_pairs={{0,1},{1,0},{2,3},{3,2},{4,5},{5,4},{6,7},{7,6},{8,9},{9,8},{10,11... | collective-permute-start | bytes 3538952 | tf_op jit(solution)/shard_map/ppermute | solution.py:241
  66.0 0.0 copy-done.6
  66.1 0.6 dynamic_slice.15.bias
  66.7 0.1 pad_add_fusion.info
  66.8 1.4 %collective-permute-done = bf16[4608,128]{1,0:T(8,128)(2,1)S(1)} collective-permute-done((bf16[4608,128]{1,0:T(8,128)(2,1)S(1)}, bf16[4608,128]{1,0:T(8,128)(2,1)S(1)}, u32[]{:S(2)}, u32[]{:S(2)}) %collective-permute-start) | collective-permute-done | bytes 1179680 | tf_op jit(solution)/shard_map/ppermute | solution.py:241
  68.2 0.0 copy-start.2
  68.2 1.0 copy-done.2
  69.2 0.0 copy-start.3
  69.2 1.3 %copy-done.3 = bf16[4608,128]{1,0:T(8,128)(2,1)S(1)} copy-done((bf16[4608,128]{1,0:T(8,128)(2,1)S(1)}, bf16[4608,128]{1,0:T(8,128)(2,1)}, u32[]{:S(2)}) %copy-start.3) | copy-done | bytes 1179672
  70.5 0.9 assemble.1
  71.4 0.0 copy-start.4
  71.4 0.6 copy-done.4
  72.1 0.0 all-gather.2.cloned.1.call-done.x_hbm
  72.1 0.0 copy-start.1
  72.1 2.2 %copy-done.1 = bf16[4,256,2048]{2,1,0:T(8,128)(2,1)S(1)} copy-done((bf16[4,256,2048]{2,1,0:T(8,128)(2,1)S(1)}, bf16[4,256,2048]{2,1,0:T(8,128)(2,1)}, u32[]{:S(2)}) %copy-start.1) | copy-done | bytes 4194328
  74.3 0.0 copy-start.5
  74.3 0.8 copy-done.5
  75.1 7.5 %project.1 = (bf16[1024,128]{1,0:T(8,128)(2,1)S(1)}, bf16[128,1024]{1,0:T(8,128)(2,1)S(1)}, bf16[1024,256]{1,0:T(8,128)(2,1)S(1)}, f32[8,1024]{1,0:T(8,128)S(1)}, bf16[4,128,384]{2,1,0:T(8,128)(2,1)S(1)}) custom-call(s32[3]{0:T(128)S(1)} %pad_add_fusion.info, f32[1]{0:T(128)} %dynamic_slice.15.bias, bf16[4,256,2048]{2,1,0:T(8,128)(2,1)S(1)} %copy-done.1, ...), custom_call_target="tpu_custom_call" | custom-call | tf_op jit(solution)/shard_map/project/pallas_call | solution.py:182
  82.6 11.0 %all_to_all.27.states_ref = bf16[4,128,384]{2,1,0:T(8,128)(2,1)S(1)} all-to-all(bf16[4,128,384]{2,1,0:T(8,128)(2,1)S(1)} %get-tuple-element.18), channel_id=1, replica_groups=mesh['x'=4,'y'=4,'z'=16,'c'=2] {'x'}, dimensions={0} | all-to-all | bytes 786432 | tf_op jit(solution)/shard_map/all_to_all | solution.py:247
  93.6 2.7 %cell.1 = bf16[4,256,256]{2,1,0:T(8,128)(2,1)S(1)} custom-call(s32[3]{0:T(128)S(1)} %pad_add_fusion.info, bf16[1024,128]{1,0:T(8,128)(2,1)S(1)} %get-tuple-element.14.q_ref, bf16[128,1024]{1,0:T(8,128)(2,1)S(1)} %get-tuple-element.15.kt_ref, bf16[1024,256]{1,0:T(8,128)(2,1)S(1)} %get-tuple-element.16.v_ref, f32[8,1024]{1,0:T(8,128)S(1)} %get-tuple-element.17.rows_ref, ...), custom_call_target="tpu_custom_call" | custom-call | tf_op jit(solution)/shard_map/cell/pallas_call | solution.py:204
  96.3 13.2 %all_to_all.28.heads_ref = bf16[4,256,256]{2,1,0:T(8,128)(2,1)S(1)} all-to-all(bf16[4,256,256]{2,1,0:T(8,128)(2,1)S(1)} %cell.1), channel_id=1, replica_groups=mesh['x'=4,'y'=4,'z'=16,'c'=2] {'y'}, dimensions={0} | all-to-all | bytes 1048576 | tf_op jit(solution)/shard_map/all_to_all | solution.py:249
  109.5 0.9 merge.1
  (3 shorter events, 0.1 us)
Async XLA Ops:
  6.5 2.9 %copy-start = (bf16[64,2048]{1,0:T(8,128)(2,1)S(1)}, bf16[64,2048]{1,0:T(8,128)(2,1)}, u32[]{:S(2)}) copy-start(bf16[64,2048]{1,0:T(8,128)(2,1)} %param.6) | copy-start | bytes 786436
  6.5 65.5 %all-gather.2.cloned.1.call-start = ((), (), s32[]{:S(2)}) async-start(), calls=%async_computation.4 | async-start | bytes 5242880 | tf_op jit(solution)/shard_map/all_gather | solution.py:237
  43.5 22.5 %copy-start.6 = (f32[4]{0:T(128)S(1)}, f32[4]{0:T(128)}, u32[]{:S(2)}) copy-start(f32[4]{0:T(128)} %param.8) | copy-start | bytes 52
  63.5 4.7 %collective-permute-start = (bf16[4608,128]{1,0:T(8,128)(2,1)S(1)}, bf16[4608,128]{1,0:T(8,128)(2,1)S(1)}, u32[]{:S(2)}, u32[]{:S(2)}) collective-permute-start(bf16[4608,128]{1,0:T(8,128)(2,1)S(1)} %bitcast.13), channel_id=1, source_target_pairs={{0,1},{1,0},{2,3},{3,2},{4,5},{5,4},{6,7},{7,6},{8,9},{9,8},{10,11... | collective-permute-start | bytes 3538952 | tf_op jit(solution)/shard_map/ppermute | solution.py:241
  68.2 1.0 copy-start.2
  69.2 1.3 %copy-start.3 = (bf16[4608,128]{1,0:T(8,128)(2,1)S(1)}, bf16[4608,128]{1,0:T(8,128)(2,1)}, u32[]{:S(2)}) copy-start(bf16[4608,128]{1,0:T(8,128)(2,1)} %copy-done.2) | copy-start | bytes 3538948
  71.4 0.6 copy-start.4
  72.1 2.2 %copy-start.1 = (bf16[4,256,2048]{2,1,0:T(8,128)(2,1)S(1)}, bf16[4,256,2048]{2,1,0:T(8,128)(2,1)}, u32[]{:S(2)}) copy-start(bf16[4,256,2048]{2,1,0:T(8,128)(2,1)} %all-gather.2.cloned.1.call-done.x_hbm) | copy-start | bytes 12582916
  74.3 0.8 copy-start.5
Sparse Core Ops, SparseCore 0:
  9.5 60.0 all-gather.1

commit v4 on v3

--- a/solution.py
+++ b/solution.py
@@ -16,6 +16,7 @@
 HALF = D // (NZ * NC)
 PIECE = HALF + 8
 EXT = DV + 128
+WIDE = 2 * DK + DV + 128
 lowest = -1e30
 
 
@@ -44,8 +45,7 @@
     return jnp.concatenate([chunk[at : at + 1, :] for at in range(QUAD // 128)], axis=1)
 
 
-def assemble_kernel(info, own_ref, other_ref, weight_ref, gate_ref):
-    core = info[0]
+def assemble(core, own_ref, other_ref, weight_ref):
     for part in range(4):
         for z in range(NZ):
             columns = pl.ds(part * 128, 128)
@@ -57,15 +57,27 @@
     second = jnp.where(core == 0, theirs, mine)
     inputs = jnp.concatenate([first[:, :HALF], second[:, :HALF]], axis=1)
     forgets = jnp.concatenate([first[:, HALF:], second[:, HALF:]], axis=1)
-    gate_ref[...] = jnp.zeros_like(gate_ref)
+    row = lax.broadcasted_iota(jnp.int32, (128, 128), 0)
     for z in range(NZ):
-        columns = pl.ds(z * 128, 128)
-        gate_ref[0:1, columns] = inputs[z : z + 1]
-        gate_ref[1:2, columns] = forgets[z : z + 1]
+        rows = jnp.where(row == 0, inputs[z : z + 1], jnp.where(row == 1, forgets[z : z + 1], 0.0))
+        columns = rows.T.astype(jnp.bfloat16).reshape(NC, HALF, 128)
+        weight_ref[z, :, :, 2 * DK + DV :] = columns
 
 
 def project_kernel(
-    info, bias, x_hbm, weight_ref, gate_ref, q_ref, kt_ref, v_ref, rows_ref, sent_ref, tokens, arrived
+    info,
+    bias,
+    x_hbm,
+    own_ref,
+    other_ref,
+    q_ref,
+    kt_ref,
+    v_ref,
+    rows_ref,
+    sent_ref,
+    weight_ref,
+    tokens,
+    arrived,
 ):
     copies = [
         pltpu.make_async_copy(x_hbm.at[block], tokens.at[block], arrived.at[block])
@@ -73,17 +85,16 @@
     ]
     for copy in copies:
         copy.start()
-    weight = weight_ref[...].reshape(D, 2 * DK + DV)
-    gate = gate_ref[...].astype(jnp.bfloat16)
+    assemble(info[0], own_ref, other_ref, weight_ref)
     pre = []
     for block in range(NY):
         copies[block].wait()
         here = pl.ds(block * TOK, TOK)
-        pre.append(dot(gate, tokens[block], ((1,), (1,))))
-        projected = dot(tokens[block], weight)
+        projected = dot(tokens[block], weight_ref[...].reshape(D, WIDE))
         q_ref[here, :] = projected[:, :DK].astype(jnp.bfloat16)
         kt_ref[:, here] = projected[:, DK : 2 * DK].T.astype(jnp.bfloat16)
-        v_ref[here, :] = projected[:, 2 * DK :].astype(jnp.bfloat16)
+        v_ref[here, :] = projected[:, 2 * DK : 2 * DK + DV].astype(jnp.bfloat16)
+        pre.append(projected[:, 2 * DK + DV :].T[:8, :])
     pre = jnp.concatenate(pre, axis=1)
 
     accepted = info[1]
@@ -166,19 +177,7 @@
     return jax.ShapeDtypeStruct(shape, dtype)
 
 
-def assemble(info, own, other, **options):
-    return pl.pallas_call(
-        assemble_kernel,
-        out_shape=(shaped(NZ, NC, HALF, 2 * DK + DV), shaped(8, D, dtype=jnp.float32)),
-        in_specs=[SMEM, VMEM, VMEM],
-        out_specs=(VMEM, VMEM),
-        compiler_params=granted(16),
-        name="assemble",
-        **options,
-    )(info, own, other)
-
-
-def project(info, bias, quad, weight, gate, **options):
+def project(info, bias, quad, own, other, **options):
     return pl.pallas_call(
         project_kernel,
         out_shape=(
@@ -191,13 +190,14 @@
         in_specs=[SMEM, SMEM, pl.BlockSpec(memory_space=pltpu.HBM), VMEM, VMEM],
         out_specs=(VMEM,) * 5,
         scratch_shapes=[
+            pltpu.VMEM((NZ, NC, HALF, WIDE), jnp.bfloat16),
             pltpu.VMEM((NY, TOK, D), jnp.bfloat16),
             pltpu.SemaphoreType.DMA((NY,)),
         ],
-        compiler_params=granted(24),
+        compiler_params=granted(49),
         name="project",
         **options,
-    )(info, bias, quad, weight, gate)
+    )(info, bias, quad, own, other)
 
 
 def cell(info, q, kt, v, rows, states, **options):
@@ -224,26 +224,48 @@
     )(heads)
 
 
-def weight_piece(proj_weight, gate_weight, x, y):
-    quarter = jnp.stack([y, H + y, 2 * H + 2 * y, 2 * H + 2 * y + 1])[x]
-    columns = lax.dynamic_slice(proj_weight, (0, quarter * 128), (HALF, 128))
-    pair = [lax.dynamic_slice(gate_weight, (0, at), (HALF, 1)) for at in (y, H + y)]
-    row = jnp.concatenate(pair, axis=0).reshape(1, 2 * HALF)
-    return jnp.concatenate([columns, row, jnp.zeros((7, 128), row.dtype)], axis=0)
+def piece_kernel(place, proj_ref, gate_ref, out_ref):
+    x, y = place[0], place[1]
+    for quarter, at in enumerate((y, H + y, 2 * H + 2 * y, 2 * H + 2 * y + 1)):
+
+        @pl.when(x == quarter)
+        def _(at=at):
+            out_ref[0, :HALF, :] = proj_ref[:, pl.ds(pl.multiple_of(at * 128, 128), 128)]
+
+    lane = lax.broadcasted_iota(jnp.int32, (HALF, 2 * H), 1)
+    gates = gate_ref[...].astype(jnp.float32)
+    inputs = jnp.sum(jnp.where(lane == y, gates, 0.0), axis=1, keepdims=True)
+    forgets = jnp.sum(jnp.where(lane == H + y, gates, 0.0), axis=1, keepdims=True)
+    both = jnp.broadcast_to(jnp.concatenate([inputs, forgets], axis=0), (128, 128))
+    row = lax.broadcasted_iota(jnp.int32, (8, 128), 0)
+    out_ref[0, HALF:, :] = jnp.where(row == 0, both.T[:8, :], 0.0).astype(jnp.bfloat16)
+    for to in range(1, NZ):
+        out_ref[to] = out_ref[0]
+
+
+def weight_piece(place, proj_weight, gate_weight, **options):
+    return pl.pallas_call(
+        piece_kernel,
+        out_shape=shaped(NZ, PIECE, 128),
+        in_specs=[SMEM, VMEM, VMEM],
+        out_specs=VMEM,
+        compiler_params=granted(8),
+        name="piece",
+        **options,
+    )(place, proj_weight, gate_weight)
 
 
 def per_device(activations, proj_weight, gate_weight, forget_bias, accepted):
     x, y, core = (lax.axis_index(a) for a in ("x", "y", "c"))
     quad = lax.all_gather(activations, "y", axis=0, tiled=True)
-    piece = weight_piece(proj_weight, gate_weight, x, y)
-    rows = lax.all_to_all(jnp.tile(piece, (NZ, 1)), "z", 0, 0, tiled=True)
-    own = lax.all_to_all(jnp.tile(rows, (NX, 1)), "x", 0, 0, tiled=True)
+    place = jnp.stack([x, y]).astype(jnp.int32)
+    rows = lax.all_to_all(weight_piece(place, proj_weight, gate_weight), "z", 0, 0, tiled=True)
+    own = lax.all_to_all(jnp.tile(rows, (NX, 1, 1)), "x", 0, 0, tiled=True)
     other = lax.ppermute(own, "c", [(0, 1), (1, 0)])
     shape = (4, NZ, PIECE, 128)
     info = jnp.stack([core, accepted[0], x]).astype(jnp.int32)
     bias = lax.dynamic_slice(forget_bias, (y,), (1,))
-    weight, gate = assemble(info, own.reshape(shape), other.reshape(shape))
-    q, kt, v, gates, sent = project(info, bias, quad, weight, gate)
+    q, kt, v, gates, sent = project(info, bias, quad, own.reshape(shape), other.reshape(shape))
     states = lax.all_to_all(sent, "x", 0, 0, tiled=True)
     out = cell(info, q, kt, v, gates, states)
     return merge(lax.all_to_all(out, "y", 0, 0, tiled=True))

time: 118 us -> 112 us (0.949)
  local copies, waits for them, and re-layouts: 8.23 us -> 1.56 us
  waiting for transfers between devices: 2.15 us -> 4.2 us
    unnamed x14 -> x5, local copies, waits for them, and re-layouts: 5.95 us -> 0.79 us
    all_gather x1, waiting for transfers between devices: 0.01 us -> 2.03 us  [per_device(): quad = lax.all_gather(activations, 'y', axis=0, tiled=True)]
    all_to_all x1, blocking collectives: 13.2 us -> 11.4 us  [per_device(): return merge(lax.all_to_all(out, 'y', 0, 0, tiled=True))]
    dynamic_slice x3 -> x0, local copies, waits for them, and re-layouts: 1.36 us -> none  [the longest x1 0.76 us: weight_piece(): lax.dynamic_slice(gate_weight, (0, at), (HALF, 1))]
  transfers between devices with their start and end apart: 2 -> 2, of which waited for: 1 -> 2; matrix products, arithmetic and copies ran while one was open for 2% -> 2% of each run, Pallas kernels for 1% -> 1%
where the time goes in v4:
time: 112 us
  blocking collectives  77.3 us (69%)
  between operations  14.1 us (13%)
  Pallas kernels  12.8 us (11%)
  waiting for transfers between devices  4.2 us (4%)
  starting transfers between devices  1.91 us (2%)
  local copies, waits for them, and re-layouts  1.56 us (1%)
    all_to_all x1, blocking collectives, per_device(): lax.all_to_all(weight_piece(place, proj_weight, gate_weight), 'z', 0, 0,...  33.8 us
    all_to_all x1, blocking collectives, per_device(): own = lax.all_to_all(jnp.tile(rows, (NX, 1, 1)), 'x', 0, 0, tiled=True)  20 us
    all_to_all x1, blocking collectives, per_device(): states = lax.all_to_all(sent, 'x', 0, 0, tiled=True)  12.1 us
    all_to_all x1, blocking collectives, per_device(): return merge(lax.all_to_all(out, 'y', 0, 0, tiled=True))  11.4 us
    pallas_call x1, Pallas kernels, project(): pl.pallas_call(project_kernel, out_shape=(shaped(QUAD, DK), shaped(DK, QU...  8.45 us
    pallas_call x1, Pallas kernels, cell(): pl.pallas_call(cell_kernel, out_shape=shaped(NY, TOK, DV), in_specs=[SMEM...  2.65 us
  transfers between devices with their start and end apart: 2, of which 2 were waited for; matrix products, arithmetic and copies ran while one was open for 2% of the time, Pallas kernels for 1%

profile of v4, /device:TPU:32, one launch (start us, length us, event | category | flops | bytes accessed | tf_op | source)
XLA Modules:
  0.0 111.9 jit_solution(3995138601226101279)
XLA Ops:
  6.5 0.0 copy-start
  6.5 0.0 all-gather.2.cloned.1.call-start
  6.5 0.7 all-gather.2.cloned.1.call-update
  7.3 0.8 copy.7.gate_ref
  8.0 0.1 pad_add_fusion.1.place
  8.1 0.0 copy-done
  8.1 0.8 piece.1
  8.9 33.8 %all_to_all.20 = bf16[16,72,128]{2,1,0:T(8,128)(2,1)S(1)} all-to-all(bf16[16,72,128]{2,1,0:T(8,128)(2,1)S(1)} %piece.1), channel_id=1, replica_groups=mesh['x'=4,'y'=4,'z'=16,'c'=2] {'z'}, dimensions={0} | all-to-all | bytes 589824 | tf_op jit(solution)/shard_map/all_to_all | solution.py:262
  42.7 0.2 tile.4
  42.8 0.0 copy-start.1
  42.9 20.0 %all_to_all.21 = bf16[64,72,128]{2,1,0:T(8,128)(2,1)S(1)} all-to-all(bf16[64,72,128]{2,1,0:T(8,128)(2,1)S(1)} %bitcast.8), channel_id=1, replica_groups=mesh['x'=4,'y'=4,'z'=16,'c'=2] {'x'}, dimensions={0} | all-to-all | bytes 2359296 | tf_op jit(solution)/shard_map/all_to_all | solution.py:263
  62.8 1.9 %collective-permute-start = (bf16[64,72,128]{2,1,0:T(8,128)(2,1)S(1)}, bf16[64,72,128]{2,1,0:T(8,128)(2,1)S(1)}, u32[]{:S(2)}, u32[]{:S(2)}) collective-permute-start(bf16[64,72,128]{2,1,0:T(8,128)(2,1)S(1)} %all_to_all.21), channel_id=1, source_target_pairs={{0,1},{1,0},{2,3},{3,2},{4,5},{5,4},{6,7},{7,6},{8,9},{9,8},{10,11... | collective-permute-start | bytes 3538952 | tf_op jit(solution)/shard_map/ppermute | solution.py:264
  65.4 0.0 copy-done.1
  65.4 0.6 dynamic_slice.3.bias
  66.0 0.1 pad_add_fusion.info
  66.1 1.5 %collective-permute-done = bf16[64,72,128]{2,1,0:T(8,128)(2,1)S(1)} collective-permute-done((bf16[64,72,128]{2,1,0:T(8,128)(2,1)S(1)}, bf16[64,72,128]{2,1,0:T(8,128)(2,1)S(1)}, u32[]{:S(2)}, u32[]{:S(2)}) %collective-permute-start) | collective-permute-done | bytes 1179680 | tf_op jit(solution)/shard_map/ppermute | solution.py:264
  67.5 2.0 %all-gather.2.cloned.1.call-done.x_hbm = bf16[4,256,2048]{2,1,0:T(8,128)(2,1)} async-done(((bf16[1,256,2048]{2,1,0:T(8,128)(2,1)}), bf16[4,256,2048]{2,1,0:T(8,128)(2,1)}) %all-gather.2.cloned.1.call-update) | async-done | bytes 4194320 | tf_op jit(solution)/shard_map/all_gather | solution.py:260
  69.6 8.5 %project.1 = (bf16[1024,128]{1,0:T(8,128)(2,1)S(1)}, bf16[128,1024]{1,0:T(8,128)(2,1)S(1)}, bf16[1024,256]{1,0:T(8,128)(2,1)S(1)}, f32[8,1024]{1,0:T(8,128)S(1)}, bf16[4,128,384]{2,1,0:T(8,128)(2,1)S(1)}) custom-call(s32[3]{0:T(128)S(1)} %pad_add_fusion.info, f32[1]{0:T(128)} %dynamic_slice.3.bias, bf16[4,256,2048]{2,1,0:T(8,128)(2,1)} %all-gather.2.cloned.1.call-done.x_hbm, ...), custom_call_target="tpu_custom_call" | custom-call | tf_op jit(solution)/shard_map/project/pallas_call | solution.py:181
  78.0 12.1 %all_to_all.22.states_ref = bf16[4,128,384]{2,1,0:T(8,128)(2,1)S(1)} all-to-all(bf16[4,128,384]{2,1,0:T(8,128)(2,1)S(1)} %get-tuple-element.14), channel_id=1, replica_groups=mesh['x'=4,'y'=4,'z'=16,'c'=2] {'x'}, dimensions={0} | all-to-all | bytes 786432 | tf_op jit(solution)/shard_map/all_to_all | solution.py:269
  90.2 2.7 %cell.1 = bf16[4,256,256]{2,1,0:T(8,128)(2,1)S(1)} custom-call(s32[3]{0:T(128)S(1)} %pad_add_fusion.info, bf16[1024,128]{1,0:T(8,128)(2,1)S(1)} %get-tuple-element.10.q_ref, bf16[128,1024]{1,0:T(8,128)(2,1)S(1)} %get-tuple-element.11.kt_ref, bf16[1024,256]{1,0:T(8,128)(2,1)S(1)} %get-tuple-element.12.v_ref, f32[8,1024]{1,0:T(8,128)S(1)} %get-tuple-element.13.rows_ref, ...), custom_call_target="tpu_custom_call" | custom-call | tf_op jit(solution)/shard_map/cell/pallas_call | solution.py:204
  92.8 11.4 %all_to_all.23.heads_ref = bf16[4,256,256]{2,1,0:T(8,128)(2,1)S(1)} all-to-all(bf16[4,256,256]{2,1,0:T(8,128)(2,1)S(1)} %cell.1), channel_id=1, replica_groups=mesh['x'=4,'y'=4,'z'=16,'c'=2] {'y'}, dimensions={0} | all-to-all | bytes 1048576 | tf_op jit(solution)/shard_map/all_to_all | solution.py:271
  104.2 0.9 merge.1
Async XLA Ops:
  6.5 1.6 %copy-start = (bf16[64,2048]{1,0:T(8,128)(2,1)S(1)}, bf16[64,2048]{1,0:T(8,128)(2,1)}, u32[]{:S(2)}) copy-start(bf16[64,2048]{1,0:T(8,128)(2,1)} %proj_ref.1) | copy-start | bytes 786436
  6.5 63.0 %all-gather.2.cloned.1.call-start = ((), (), s32[]{:S(2)}) async-start(), calls=%async_computation.4 | async-start | bytes 5242880 | tf_op jit(solution)/shard_map/all_gather | solution.py:260
  42.8 22.5 %copy-start.1 = (f32[4]{0:T(128)S(1)}, f32[4]{0:T(128)}, u32[]{:S(2)}) copy-start(f32[4]{0:T(128)} %param.8) | copy-start | bytes 52
  62.8 4.7 %collective-permute-start = (bf16[64,72,128]{2,1,0:T(8,128)(2,1)S(1)}, bf16[64,72,128]{2,1,0:T(8,128)(2,1)S(1)}, u32[]{:S(2)}, u32[]{:S(2)}) collective-permute-start(bf16[64,72,128]{2,1,0:T(8,128)(2,1)S(1)} %all_to_all.21), channel_id=1, source_target_pairs={{0,1},{1,0},{2,3},{3,2},{4,5},{5,4},{6,7},{7,6},{8,9},{9,8},{10,11... | collective-permute-start | bytes 3538952 | tf_op jit(solution)/shard_map/ppermute | solution.py:264
Sparse Core Ops, SparseCore 0:
  9.5 60.0 all-gather.1

commit v5 on v4

--- a/solution.py
+++ b/solution.py
@@ -14,6 +14,7 @@
 NX, NY, NZ, NC = 4, 4, 16, 2
 QUAD = NY * TOK
 HALF = D // (NZ * NC)
+CUT = 160
 PIECE = HALF + 8
 EXT = DV + 128
 WIDE = 2 * DK + DV + 128
@@ -67,7 +68,11 @@
 def project_kernel(
     info,
     bias,
-    x_hbm,
+    x_ref,
+    near_ref,
+    far_ref,
+    head_ref,
+    tail_ref,
     own_ref,
     other_ref,
     q_ref,
@@ -76,34 +81,25 @@
     rows_ref,
     sent_ref,
     weight_ref,
-    tokens,
-    arrived,
+    pre_ref,
+    scaling_ref,
 ):
-    copies = [
-        pltpu.make_async_copy(x_hbm.at[block], tokens.at[block], arrived.at[block])
-        for block in range(NY)
-    ]
-    for copy in copies:
-        copy.start()
     assemble(info[0], own_ref, other_ref, weight_ref)
-    pre = []
-    for block in range(NY):
-        copies[block].wait()
-        here = pl.ds(block * TOK, TOK)
-        projected = dot(tokens[block], weight_ref[...].reshape(D, WIDE))
-        q_ref[here, :] = projected[:, :DK].astype(jnp.bfloat16)
-        kt_ref[:, here] = projected[:, DK : 2 * DK].T.astype(jnp.bfloat16)
-        v_ref[here, :] = projected[:, 2 * DK : 2 * DK + DV].astype(jnp.bfloat16)
-        pre.append(projected[:, 2 * DK + DV :].T[:8, :])
-    pre = jnp.concatenate(pre, axis=1)
-
-    accepted = info[1]
-    positions = info[2] * QUAD + lax.broadcasted_iota(jnp.int32, (1, QUAD), 1)
-    live = positions < accepted
-    forget_pre = pre[1:2, :] + bias[0]
+    across = jnp.concatenate([head_ref[...], tail_ref[...]], axis=0)
+    tokens = {0: x_ref[0], 1: near_ref[...], 3: far_ref[...], 2: across}
+    places = {
+        swap: pl.ds(pl.multiple_of(jnp.bitwise_xor(info[3], swap) * TOK, TOK), TOK)
+        for swap in tokens
+    }
+    for swap, part in tokens.items():
+        gates = dot(part, weight_ref[:, :, :, 2 * DK + DV :].reshape(D, 128))
+        pre_ref[:, places[swap]] = gates.T[:8, :]
+
+    live = info[2] * QUAD + lax.broadcasted_iota(jnp.int32, (1, QUAD), 1) < info[1]
+    forget_pre = pre_ref[1:2, :] + bias[0]
     log_sigmoid = jnp.minimum(forget_pre, 0.0) - jnp.log1p(jnp.exp(-jnp.abs(forget_pre)))
     log_forget = jnp.where(live, log_sigmoid, 0.0)
-    log_input = jnp.where(live, pre[0:1, :], lowest)
+    log_input = jnp.where(live, pre_ref[0:1, :], lowest)
     decay_sum = scan_row(log_forget, jnp.add, 0.0)
     relative = log_input - decay_sum
     running_top = scan_row(relative, jnp.maximum, 2 * lowest)
@@ -112,10 +108,22 @@
     rows_ref[...] = jnp.concatenate(
         [relative, running_top, jnp.zeros((6, QUAD), jnp.float32)], axis=0
     )
-    scaling = jnp.where(live, jnp.exp(relative - last_top), 0.0)
-    weighted = kt_ref[...].astype(jnp.float32) * scaling
-    normal = jnp.sum(weighted, axis=1, keepdims=True)
-    memory = dot(weighted.astype(jnp.bfloat16), v_ref[...])
+    scaling_ref[0:1, :] = jnp.where(live, jnp.exp(relative - last_top), 0.0)
+
+    memory = jnp.zeros((DK, DV), jnp.float32)
+    normal = jnp.zeros((DK, TOK), jnp.float32)
+    for swap, part in tokens.items():
+        here = places[swap]
+        projected = dot(part, weight_ref[:, :, :, : 2 * DK + DV].reshape(D, 2 * DK + DV))
+        keys = projected[:, DK : 2 * DK].astype(jnp.bfloat16).T
+        values = projected[:, 2 * DK :].astype(jnp.bfloat16)
+        q_ref[here, :] = projected[:, :DK].astype(jnp.bfloat16)
+        kt_ref[:, here] = keys
+        v_ref[here, :] = values
+        weighted = keys.astype(jnp.float32) * scaling_ref[0:1, here]
+        normal = normal + weighted
+        memory = memory + dot(weighted.astype(jnp.bfloat16), values)
+    normal = jnp.sum(normal, axis=1, keepdims=True)
     lane = lax.broadcasted_iota(jnp.int32, (DK, 128), 1)
     logs = jnp.where(lane == 0, normal, 0.0)
     for at, value in enumerate((*split3(total), *split3(total + last_top))):
@@ -177,7 +185,7 @@
     return jax.ShapeDtypeStruct(shape, dtype)
 
 
-def project(info, bias, quad, own, other, **options):
+def project(info, bias, tokens, own, other, **options):
     return pl.pallas_call(
         project_kernel,
         out_shape=(
@@ -187,17 +195,17 @@
             shaped(8, QUAD, dtype=jnp.float32),
             shaped(NX, DK, EXT),
         ),
-        in_specs=[SMEM, SMEM, pl.BlockSpec(memory_space=pltpu.HBM), VMEM, VMEM],
+        in_specs=[SMEM, SMEM] + [VMEM] * 7,
         out_specs=(VMEM,) * 5,
         scratch_shapes=[
             pltpu.VMEM((NZ, NC, HALF, WIDE), jnp.bfloat16),
-            pltpu.VMEM((NY, TOK, D), jnp.bfloat16),
-            pltpu.SemaphoreType.DMA((NY,)),
+            pltpu.VMEM((8, QUAD), jnp.float32),
+            pltpu.VMEM((8, QUAD), jnp.float32),
         ],
-        compiler_params=granted(49),
+        compiler_params=granted(24),
         name="project",
         **options,
-    )(info, bias, quad, own, other)
+    )(info, bias, *tokens, own, other)
 
 
 def cell(info, q, kt, v, rows, states, **options):
@@ -255,17 +263,27 @@
     )(place, proj_weight, gate_weight)
 
 
+def swap_along(array, axis, swap):
+    return lax.ppermute(array, axis, [(i, i ^ swap) for i in range(4)])
+
+
 def per_device(activations, proj_weight, gate_weight, forget_bias, accepted):
     x, y, core = (lax.axis_index(a) for a in ("x", "y", "c"))
-    quad = lax.all_gather(activations, "y", axis=0, tiled=True)
+    own_tokens = activations[0]
+    near = swap_along(own_tokens, "y", 1)
+    far = swap_along(own_tokens, "y", 3)
+    head = swap_along(near[:CUT], "y", 3)
+    tail = swap_along(far[CUT:], "y", 1)
     place = jnp.stack([x, y]).astype(jnp.int32)
-    rows = lax.all_to_all(weight_piece(place, proj_weight, gate_weight), "z", 0, 0, tiled=True)
-    own = lax.all_to_all(jnp.tile(rows, (NX, 1, 1)), "x", 0, 0, tiled=True)
+    rows = lax.all_to_all(weight_piece(place, proj_weight, gate_weight), "z", 0, 0)
+    own = lax.all_to_all(jnp.tile(rows.reshape(1, NZ * PIECE, 128), (NX, 1, 1)), "x", 0, 0)
+    own, head, tail = lax.optimization_barrier((own.reshape(NX * NZ * PIECE, 128), head, tail))
     other = lax.ppermute(own, "c", [(0, 1), (1, 0)])
     shape = (4, NZ, PIECE, 128)
-    info = jnp.stack([core, accepted[0], x]).astype(jnp.int32)
+    info = jnp.stack([core, accepted[0], x, y]).astype(jnp.int32)
     bias = lax.dynamic_slice(forget_bias, (y,), (1,))
-    q, kt, v, gates, sent = project(info, bias, quad, own.reshape(shape), other.reshape(shape))
+    tokens = (activations, near, far, head, tail)
+    q, kt, v, gates, sent = project(info, bias, tokens, own.reshape(shape), other.reshape(shape))
     states = lax.all_to_all(sent, "x", 0, 0, tiled=True)
     out = cell(info, q, kt, v, gates, states)
     return merge(lax.all_to_all(out, "y", 0, 0, tiled=True))

time: 112 us -> 107 us (0.955)
  blocking collectives: 77.3 us -> 24.6 us
  starting transfers between devices: 1.91 us -> 36 us
  waiting for transfers between devices: 4.2 us -> 25.6 us
  between operations: 14.1 us -> 0.75 us
  local copies, waits for them, and re-layouts: 1.56 us -> 7.29 us
    all_to_all x2 -> x0, blocking collectives: 53.7 us -> none  [the longest x1 33.8 us: per_device(): lax.all_to_all(weight_piece(place, proj_weight, gate_weight), 'z', 0, 0,...]
    all_to_all x0 -> x2, starting transfers between devices: none -> 19.5 us  [the longest x1 15.2 us: per_device(): lax.all_to_all(weight_piece(place, proj_weight, gate_weight), 'z', 0, 0)]
    ppermute x0 -> x4, starting transfers between devices: none -> 14.5 us  [swap_along(): return lax.ppermute(array, axis, [(i, i ^ swap) for i in range(4)])]
    ppermute x0 -> x4, waiting for transfers between devices: none -> 12.8 us  [swap_along(): return lax.ppermute(array, axis, [(i, i ^ swap) for i in range(4)])]
    all_to_all x0 -> x2, waiting for transfers between devices: none -> 11.2 us  [the longest x1 11.2 us: per_device(): lax.all_to_all(weight_piece(place, proj_weight, gate_weight), 'z', 0, 0)]
    unnamed x5 -> x13, local copies, waits for them, and re-layouts: 0.79 us -> 5.43 us
    all_gather x1 -> x0, waiting for transfers between devices: 2.03 us -> none  [per_device(): quad = lax.all_gather(activations, 'y', axis=0, tiled=True)]
    pallas_call x1, Pallas kernels: 8.45 us -> 6.89 us  [project(): pl.pallas_call(project_kernel, out_shape=(shaped(QUAD, DK), shaped(DK, QU...]
  transfers between devices with their start and end apart: 2 -> 7, of which waited for: 2 -> 5; matrix products, arithmetic and copies ran while one was open for 2% -> 2% of each run, Pallas kernels for 1% -> 0%
where the time goes in v5:
time: 107 us; the launch traced here: 106 us
  starting transfers between devices  36 us (34%)
  waiting for transfers between devices  25.6 us (24%)
  blocking collectives  24.6 us (23%)
  Pallas kernels  11.9 us (11%)
  local copies, waits for them, and re-layouts  7.29 us (7%)
    all_to_all x1, starting transfers between devices, per_device(): lax.all_to_all(weight_piece(place, proj_weight, gate_weight), 'z', 0, 0)  15.2 us
    ppermute x4, starting transfers between devices, swap_along(): return lax.ppermute(array, axis, [(i, i ^ swap) for i in range(4)])  14.5 us
    ppermute x4, waiting for transfers between devices, swap_along(): return lax.ppermute(array, axis, [(i, i ^ swap) for i in range(4)])  12.8 us
    all_to_all x1, blocking collectives, per_device(): states = lax.all_to_all(sent, 'x', 0, 0, tiled=True)  12.5 us
    all_to_all x1, blocking collectives, per_device(): return merge(lax.all_to_all(out, 'y', 0, 0, tiled=True))  12.1 us
    all_to_all x1, waiting for transfers between devices, per_device(): lax.all_to_all(weight_piece(place, proj_weight, gate_weight), 'z', 0, 0)  11.2 us
    pallas_call x1, Pallas kernels, project(): pl.pallas_call(project_kernel, out_shape=(shaped(QUAD, DK), shaped(DK, QU...  6.89 us
    unnamed x13, local copies, waits for them, and re-layouts  5.43 us
  transfers between devices with their start and end apart: 7, of which 5 were waited for; matrix products, arithmetic and copies ran while one was open for 2% of the time, Pallas kernels for 0%

profile of v5, /device:TPU:32, one launch (start us, length us, event | category | flops | bytes accessed | tf_op | source)
XLA Modules:
  0.0 106.2 jit_solution(7839732114401210182)
XLA Ops:
  0.0 0.8 copy.6.gate_ref
  0.8 0.1 pad_add_fusion.1.place
  0.9 0.0 copy-start.4
  0.9 0.9 copy-done.4
  1.8 1.5 %piece.1 = bf16[16,72,128]{2,1,0:T(8,128)(2,1)} custom-call(s32[2]{0:T(128)S(1)} %pad_add_fusion.1.place, bf16[64,2048]{1,0:T(8,128)(2,1)S(1)} %copy-done.4, bf16[64,8]{1,0:T(8,128)(2,1)S(1)} %copy.6.gate_ref), custom_call_target="tpu_custom_call" | custom-call | tf_op jit(solution)/shard_map/piece/pallas_call | solution.py:255
  3.3 15.2 %all-to-all-start = ((bf16[16,72,128]{2,1,0:T(8,128)(2,1)}), bf16[16,72,128]{2,1,0:T(8,128)(2,1)S(1)}, u32[]{:S(2)}, u32[]{:S(2)}) async-start(bf16[16,72,128]{2,1,0:T(8,128)(2,1)} %piece.1), calls=%async_computation | async-start | bytes 589824 | tf_op jit(solution)/shard_map/all_to_all | solution.py:278
  18.5 3.5 %collective-permute-start = (bf16[256,2048]{1,0:T(8,128)(2,1)}, bf16[256,2048]{1,0:T(8,128)(2,1)S(1)}, u32[]{:S(2)}, u32[]{:S(2)}) collective-permute-start(bf16[256,2048]{1,0:T(8,128)(2,1)} %bitcast.3), channel_id=1, source_target_pairs={{0,32},{32,0},{64,96},{96,64},{1,33},{33,1},{65,97},{97,65},{2,34}... | collective-permute-start | bytes 3145736 | tf_op jit(solution)/shard_map/ppermute | solution.py:267
  22.0 4.1 %collective-permute-start.1 = (bf16[256,2048]{1,0:T(8,128)(2,1)}, bf16[256,2048]{1,0:T(8,128)(2,1)S(1)}, u32[]{:S(2)}, u32[]{:S(2)}) collective-permute-start(bf16[256,2048]{1,0:T(8,128)(2,1)} %bitcast.3), channel_id=1, source_target_pairs={{0,96},{32,64},{64,32},{96,0},{1,97},{33,65},{65,33},{97,1},{2,98}... | collective-permute-start | bytes 3145736 | tf_op jit(solution)/shard_map/ppermute | solution.py:267
  26.1 11.2 %all-to-all-done = bf16[16,72,128]{2,1,0:T(8,128)(2,1)S(1)} async-done(((bf16[16,72,128]{2,1,0:T(8,128)(2,1)}), bf16[16,72,128]{2,1,0:T(8,128)(2,1)S(1)}, u32[]{:S(2)}, u32[]{:S(2)}) %all-to-all-start) | async-done | bytes 294944 | tf_op jit(solution)/shard_map/all_to_all | solution.py:278
  37.3 1.2 %tile.9 = bf16[4,1152,128]{2,1,0:T(8,128)(2,1)} broadcast(bf16[1152,128]{1,0:T(8,128)(2,1)S(1)} %bitcast.10), dimensions={1,2} | broadcast | bytes 1474560 | tf_op jit(solution)/shard_map/tile | solution.py:279
  38.5 4.3 %all-to-all-start.1 = ((bf16[4,1152,128]{2,1,0:T(8,128)(2,1)}), bf16[4,1152,128]{2,1,0:T(8,128)(2,1)S(1)}, u32[]{:S(2)}, u32[]{:S(2)}) async-start(bf16[4,1152,128]{2,1,0:T(8,128)(2,1)} %tile.9), calls=%async_computation.1 | async-start | bytes 2359296 | tf_op jit(solution)/shard_map/all_to_all | solution.py:279
  42.8 0.0 copy-start.5
  42.8 2.2 %collective-permute-done.near_ref = bf16[256,2048]{1,0:T(8,128)(2,1)S(1)} collective-permute-done((bf16[256,2048]{1,0:T(8,128)(2,1)}, bf16[256,2048]{1,0:T(8,128)(2,1)S(1)}, u32[]{:S(2)}, u32[]{:S(2)}) %collective-permute-start) | collective-permute-done | bytes 1048608 | tf_op jit(solution)/shard_map/ppermute | solution.py:267
  45.0 4.9 %collective-permute-start.2 = (bf16[160,2048]{1,0:T(8,128)(2,1)S(1)}, bf16[160,2048]{1,0:T(8,128)(2,1)S(1)}, u32[]{:S(2)}, u32[]{:S(2)}) collective-permute-start(bf16[160,2048]{1,0:T(8,128)(2,1)S(1)} %slice.8), channel_id=1, source_target_pairs={{0,96},{32,64},{64,32},{96,0},{1,97},{33,65},{65,33},{97,1},{2,98}... | collective-permute-start | bytes 1966088 | tf_op jit(solution)/shard_map/ppermute | solution.py:267
  49.9 0.0 collective-permute-done.1.far_ref
  50.0 2.0 %collective-permute-start.3 = (bf16[96,2048]{1,0:T(8,128)(2,1)S(1)}, bf16[96,2048]{1,0:T(8,128)(2,1)S(1)}, u32[]{:S(2)}, u32[]{:S(2)}) collective-permute-start(bf16[96,2048]{1,0:T(8,128)(2,1)S(1)} %slice.9), channel_id=1, source_target_pairs={{0,32},{32,0},{64,96},{96,64},{1,33},{33,1},{65,97},{97,65},{2,34}... | collective-permute-start | bytes 1179656 | tf_op jit(solution)/shard_map/ppermute | solution.py:267
  52.0 8.9 %collective-permute-done.3.tail_ref = bf16[96,2048]{1,0:T(8,128)(2,1)S(1)} collective-permute-done((bf16[96,2048]{1,0:T(8,128)(2,1)S(1)}, bf16[96,2048]{1,0:T(8,128)(2,1)S(1)}, u32[]{:S(2)}, u32[]{:S(2)}) %collective-permute-start.3) | collective-permute-done | bytes 393248 | tf_op jit(solution)/shard_map/ppermute | solution.py:267
  61.0 0.0 copy-start.2
  61.0 0.7 copy-done.2
  61.7 1.7 %collective-permute-done.2.head_ref = bf16[160,2048]{1,0:T(8,128)(2,1)S(1)} collective-permute-done((bf16[160,2048]{1,0:T(8,128)(2,1)S(1)}, bf16[160,2048]{1,0:T(8,128)(2,1)S(1)}, u32[]{:S(2)}, u32[]{:S(2)}) %collective-permute-start.2) | collective-permute-done | bytes 655392 | tf_op jit(solution)/shard_map/ppermute | solution.py:267
  63.4 0.0 copy-start
  63.4 0.9 copy-done
  64.3 0.0 all-to-all-done.1
  64.3 1.9 %collective-permute-start.4 = (bf16[4608,128]{1,0:T(8,128)(2,1)S(1)}, bf16[4608,128]{1,0:T(8,128)(2,1)}, u32[]{:S(2)}, u32[]{:S(2)}) collective-permute-start(bf16[4608,128]{1,0:T(8,128)(2,1)S(1)} %bitcast.8), channel_id=1, source_target_pairs={{0,1},{1,0},{2,3},{3,2},{4,5},{5,4},{6,7},{7,6},{8,9},{9,8},{10,11... | collective-permute-start | bytes 3538952 | tf_op jit(solution)/shard_map/ppermute | solution.py:281
  66.9 0.0 copy-done.5
  66.9 0.6 dynamic_slice.3.bias
  67.5 0.1 pad_add_fusion.info
  67.6 1.6 %collective-permute-done.4 = bf16[4608,128]{1,0:T(8,128)(2,1)} collective-permute-done((bf16[4608,128]{1,0:T(8,128)(2,1)S(1)}, bf16[4608,128]{1,0:T(8,128)(2,1)}, u32[]{:S(2)}, u32[]{:S(2)}) %collective-permute-start.4) | collective-permute-done | bytes 1179680 | tf_op jit(solution)/shard_map/ppermute | solution.py:281
  69.2 0.0 copy-start.1
  69.2 1.1 %copy-done.1 = bf16[160,2048]{1,0:T(8,128)(2,1)S(1)} copy-done((bf16[160,2048]{1,0:T(8,128)(2,1)S(1)}, bf16[160,2048]{1,0:T(8,128)(2,1)}, u32[]{:S(2)}) %copy-start.1) | copy-done | bytes 655384
  70.3 0.0 copy-start.3
  70.3 1.0 copy-done.3
  71.3 6.9 %project.1 = (bf16[1024,128]{1,0:T(8,128)(2,1)S(1)}, bf16[128,1024]{1,0:T(8,128)(2,1)S(1)}, bf16[1024,256]{1,0:T(8,128)(2,1)S(1)}, f32[8,1024]{1,0:T(8,128)S(1)}, bf16[4,128,384]{2,1,0:T(8,128)(2,1)S(1)}) custom-call(s32[4]{0:T(128)S(1)} %pad_add_fusion.info, f32[1]{0:T(128)} %dynamic_slice.3.bias, bf16[1,256,2048]{2,1,0:T(8,128)(2,1)} %x_ref.1, ...), custom_call_target="tpu_custom_call" | custom-call | tf_op jit(solution)/shard_map/project/pallas_call | solution.py:189
  78.2 12.5 %all_to_all.20.states_ref = bf16[4,128,384]{2,1,0:T(8,128)(2,1)S(1)} all-to-all(bf16[4,128,384]{2,1,0:T(8,128)(2,1)S(1)} %get-tuple-element.20), channel_id=1, replica_groups=mesh['x'=4,'y'=4,'z'=16,'c'=2] {'x'}, dimensions={0} | all-to-all | bytes 786432 | tf_op jit(solution)/shard_map/all_to_all | solution.py:287
  90.6 2.6 %cell.1 = bf16[4,256,256]{2,1,0:T(8,128)(2,1)S(1)} custom-call(s32[4]{0:T(128)S(1)} %pad_add_fusion.info, bf16[1024,128]{1,0:T(8,128)(2,1)S(1)} %get-tuple-element.16.q_ref, bf16[128,1024]{1,0:T(8,128)(2,1)S(1)} %get-tuple-element.17.kt_ref, bf16[1024,256]{1,0:T(8,128)(2,1)S(1)} %get-tuple-element.18.v_ref, f32[8,1024]{1,0:T(8,128)S(1)} %get-tuple-element.19.rows_ref, ...), custom_call_target="tpu_custom_call" | custom-call | tf_op jit(solution)/shard_map/cell/pallas_call | solution.py:212
  93.3 12.1 %all_to_all.21.heads_ref = bf16[4,256,256]{2,1,0:T(8,128)(2,1)S(1)} all-to-all(bf16[4,256,256]{2,1,0:T(8,128)(2,1)S(1)} %cell.1), channel_id=1, replica_groups=mesh['x'=4,'y'=4,'z'=16,'c'=2] {'y'}, dimensions={0} | all-to-all | bytes 1048576 | tf_op jit(solution)/shard_map/all_to_all | solution.py:289
  105.3 0.9 merge.1
  (2 shorter events, 0.1 us)
Async XLA Ops:
  0.9 1.0 copy-start.4
  3.3 34.0 %all-to-all-start = ((bf16[16,72,128]{2,1,0:T(8,128)(2,1)}), bf16[16,72,128]{2,1,0:T(8,128)(2,1)S(1)}, u32[]{:S(2)}, u32[]{:S(2)}) async-start(bf16[16,72,128]{2,1,0:T(8,128)(2,1)} %piece.1), calls=%async_computation | async-start | bytes 589824 | tf_op jit(solution)/shard_map/all_to_all | solution.py:278
  18.5 26.4 %collective-permute-start = (bf16[256,2048]{1,0:T(8,128)(2,1)}, bf16[256,2048]{1,0:T(8,128)(2,1)S(1)}, u32[]{:S(2)}, u32[]{:S(2)}) collective-permute-start(bf16[256,2048]{1,0:T(8,128)(2,1)} %bitcast.3), channel_id=1, source_target_pairs={{0,32},{32,0},{64,96},{96,64},{1,33},{33,1},{65,97},{97,65},{2,34}... | collective-permute-start | bytes 3145736 | tf_op jit(solution)/shard_map/ppermute | solution.py:267
  22.0 27.9 %collective-permute-start.1 = (bf16[256,2048]{1,0:T(8,128)(2,1)}, bf16[256,2048]{1,0:T(8,128)(2,1)S(1)}, u32[]{:S(2)}, u32[]{:S(2)}) collective-permute-start(bf16[256,2048]{1,0:T(8,128)(2,1)} %bitcast.3), channel_id=1, source_target_pairs={{0,96},{32,64},{64,32},{96,0},{1,97},{33,65},{65,33},{97,1},{2,98}... | collective-permute-start | bytes 3145736 | tf_op jit(solution)/shard_map/ppermute | solution.py:267
  38.5 25.8 %all-to-all-start.1 = ((bf16[4,1152,128]{2,1,0:T(8,128)(2,1)}), bf16[4,1152,128]{2,1,0:T(8,128)(2,1)S(1)}, u32[]{:S(2)}, u32[]{:S(2)}) async-start(bf16[4,1152,128]{2,1,0:T(8,128)(2,1)} %tile.9), calls=%async_computation.1 | async-start | bytes 2359296 | tf_op jit(solution)/shard_map/all_to_all | solution.py:279
  42.8 24.1 %copy-start.5 = (f32[4]{0:T(128)S(1)}, f32[4]{0:T(128)}, u32[]{:S(2)}) copy-start(f32[4]{0:T(128)} %param.8) | copy-start | bytes 52
  45.0 18.4 %collective-permute-start.2 = (bf16[160,2048]{1,0:T(8,128)(2,1)S(1)}, bf16[160,2048]{1,0:T(8,128)(2,1)S(1)}, u32[]{:S(2)}, u32[]{:S(2)}) collective-permute-start(bf16[160,2048]{1,0:T(8,128)(2,1)S(1)} %slice.8), channel_id=1, source_target_pairs={{0,96},{32,64},{64,32},{96,0},{1,97},{33,65},{65,33},{97,1},{2,98}... | collective-permute-start | bytes 1966088 | tf_op jit(solution)/shard_map/ppermute | solution.py:267
  50.0 11.0 %collective-permute-start.3 = (bf16[96,2048]{1,0:T(8,128)(2,1)S(1)}, bf16[96,2048]{1,0:T(8,128)(2,1)S(1)}, u32[]{:S(2)}, u32[]{:S(2)}) collective-permute-start(bf16[96,2048]{1,0:T(8,128)(2,1)S(1)} %slice.9), channel_id=1, source_target_pairs={{0,32},{32,0},{64,96},{96,64},{1,33},{33,1},{65,97},{97,65},{2,34}... | collective-permute-start | bytes 1179656 | tf_op jit(solution)/shard_map/ppermute | solution.py:267
  61.0 0.7 copy-start.2
  63.4 0.9 copy-start
  64.3 4.9 %collective-permute-start.4 = (bf16[4608,128]{1,0:T(8,128)(2,1)S(1)}, bf16[4608,128]{1,0:T(8,128)(2,1)}, u32[]{:S(2)}, u32[]{:S(2)}) collective-permute-start(bf16[4608,128]{1,0:T(8,128)(2,1)S(1)} %bitcast.8), channel_id=1, source_target_pairs={{0,1},{1,0},{2,3},{3,2},{4,5},{5,4},{6,7},{7,6},{8,9},{9,8},{10,11... | collective-permute-start | bytes 3538952 | tf_op jit(solution)/shard_map/ppermute | solution.py:281
  69.2 1.1 %copy-start.1 = (bf16[160,2048]{1,0:T(8,128)(2,1)S(1)}, bf16[160,2048]{1,0:T(8,128)(2,1)}, u32[]{:S(2)}) copy-start(bf16[160,2048]{1,0:T(8,128)(2,1)} %copy-done) | copy-start | bytes 1966084
  70.3 1.0 copy-start.3

commit v6 on v5

--- a/solution.py
+++ b/solution.py
@@ -202,7 +202,7 @@
             pltpu.VMEM((8, QUAD), jnp.float32),
             pltpu.VMEM((8, QUAD), jnp.float32),
         ],
-        compiler_params=granted(24),
+        compiler_params=granted(48),
         name="project",
         **options,
     )(info, bias, *tokens, own, other)
@@ -240,13 +240,13 @@
         def _(at=at):
             out_ref[0, :HALF, :] = proj_ref[:, pl.ds(pl.multiple_of(at * 128, 128), 128)]
 
-    lane = lax.broadcasted_iota(jnp.int32, (HALF, 2 * H), 1)
     gates = gate_ref[...].astype(jnp.float32)
-    inputs = jnp.sum(jnp.where(lane == y, gates, 0.0), axis=1, keepdims=True)
-    forgets = jnp.sum(jnp.where(lane == H + y, gates, 0.0), axis=1, keepdims=True)
-    both = jnp.broadcast_to(jnp.concatenate([inputs, forgets], axis=0), (128, 128))
+    column = lax.broadcasted_iota(jnp.int32, (2 * H, HALF), 0)
+    inputs = jnp.sum(jnp.where(column == y, gates, 0.0), axis=0, keepdims=True)
+    forgets = jnp.sum(jnp.where(column == H + y, gates, 0.0), axis=0, keepdims=True)
+    both = jnp.concatenate([inputs, forgets], axis=1)
     row = lax.broadcasted_iota(jnp.int32, (8, 128), 0)
-    out_ref[0, HALF:, :] = jnp.where(row == 0, both.T[:8, :], 0.0).astype(jnp.bfloat16)
+    out_ref[0, HALF:, :] = jnp.where(row == 0, both, 0.0).astype(jnp.bfloat16)
     for to in range(1, NZ):
         out_ref[to] = out_ref[0]
 
@@ -260,7 +260,7 @@
         compiler_params=granted(8),
         name="piece",
         **options,
-    )(place, proj_weight, gate_weight)
+    )(place, proj_weight, gate_weight.T)
 
 
 def swap_along(array, axis, swap):

time: 107 us -> 106 us (level)
  local copies, waits for them, and re-layouts: 7.29 us -> 5.45 us
    unnamed x13 -> x12, local copies, waits for them, and re-layouts: 5.43 us -> 3.57 us
where the time goes in v6:
time: 106 us; the launch traced here: 105 us
  starting transfers between devices  36 us (34%)
  waiting for transfers between devices  26.6 us (25%)
  blocking collectives  24.6 us (23%)
  Pallas kernels  11.8 us (11%)
  local copies, waits for them, and re-layouts  5.45 us (5%)
    all_to_all x1, starting transfers between devices, per_device(): lax.all_to_all(weight_piece(place, proj_weight, gate_weight), 'z', 0, 0)  15.2 us
    ppermute x4, starting transfers between devices, swap_along(): return lax.ppermute(array, axis, [(i, i ^ swap) for i in range(4)])  14.5 us
    ppermute x4, waiting for transfers between devices, swap_along(): return lax.ppermute(array, axis, [(i, i ^ swap) for i in range(4)])  13.6 us
    all_to_all x1, blocking collectives, per_device(): states = lax.all_to_all(sent, 'x', 0, 0, tiled=True)  12.5 us
    all_to_all x1, blocking collectives, per_device(): return merge(lax.all_to_all(out, 'y', 0, 0, tiled=True))  12.1 us
    all_to_all x1, waiting for transfers between devices, per_device(): lax.all_to_all(weight_piece(place, proj_weight, gate_weight), 'z', 0, 0)  11.2 us
    pallas_call x1, Pallas kernels, project(): pl.pallas_call(project_kernel, out_shape=(shaped(QUAD, DK), shaped(DK, QU...  6.92 us
    all_to_all x1, starting transfers between devices, per_device(): lax.all_to_all(jnp.tile(rows.reshape(1, NZ * PIECE, 128), (NX, 1, 1)), 'x...  4.29 us
  transfers between devices with their start and end apart: 7, of which 5 were waited for; matrix products, arithmetic and copies ran while one was open for 2% of the time, Pallas kernels for 0%

profile of v6, /device:TPU:32, one launch (start us, length us, event | category | flops | bytes accessed | tf_op | source)
XLA Modules:
  0.0 105.2 jit_solution(15896181569774600409)
XLA Ops:
  0.0 0.1 pad_add_fusion.1.place
  0.1 0.0 copy-start.3
  0.1 0.9 copy-done.3
  1.0 0.0 copy-start.4
  1.0 0.7 copy-done.4
  1.7 1.4 %piece.1 = bf16[16,72,128]{2,1,0:T(8,128)(2,1)} custom-call(s32[2]{0:T(128)S(1)} %pad_add_fusion.1.place, bf16[64,2048]{1,0:T(8,128)(2,1)S(1)} %copy-done.3, bf16[8,64]{1,0:T(8,128)(2,1)S(1)} %bitcast.11), custom_call_target="tpu_custom_call" | custom-call | tf_op jit(solution)/shard_map/piece/pallas_call | solution.py:255
  3.1 15.2 %all-to-all-start = ((bf16[16,72,128]{2,1,0:T(8,128)(2,1)}), bf16[16,72,128]{2,1,0:T(8,128)(2,1)S(1)}, u32[]{:S(2)}, u32[]{:S(2)}) async-start(bf16[16,72,128]{2,1,0:T(8,128)(2,1)} %piece.1), calls=%async_computation | async-start | bytes 589824 | tf_op jit(solution)/shard_map/all_to_all | solution.py:278
  18.3 3.5 %collective-permute-start = (bf16[256,2048]{1,0:T(8,128)(2,1)}, bf16[256,2048]{1,0:T(8,128)(2,1)S(1)}, u32[]{:S(2)}, u32[]{:S(2)}) collective-permute-start(bf16[256,2048]{1,0:T(8,128)(2,1)} %bitcast.9), channel_id=1, source_target_pairs={{0,32},{32,0},{64,96},{96,64},{1,33},{33,1},{65,97},{97,65},{2,34}... | collective-permute-start | bytes 3145736 | tf_op jit(solution)/shard_map/ppermute | solution.py:267
  21.8 4.1 %collective-permute-start.1 = (bf16[256,2048]{1,0:T(8,128)(2,1)}, bf16[256,2048]{1,0:T(8,128)(2,1)S(1)}, u32[]{:S(2)}, u32[]{:S(2)}) collective-permute-start(bf16[256,2048]{1,0:T(8,128)(2,1)} %bitcast.10), channel_id=1, source_target_pairs={{0,96},{32,64},{64,32},{96,0},{1,97},{33,65},{65,33},{97,1},{2,98}... | collective-permute-start | bytes 3145736 | tf_op jit(solution)/shard_map/ppermute | solution.py:267
  25.9 11.2 %all-to-all-done = bf16[16,72,128]{2,1,0:T(8,128)(2,1)S(1)} async-done(((bf16[16,72,128]{2,1,0:T(8,128)(2,1)}), bf16[16,72,128]{2,1,0:T(8,128)(2,1)S(1)}, u32[]{:S(2)}, u32[]{:S(2)}) %all-to-all-start) | async-done | bytes 294944 | tf_op jit(solution)/shard_map/all_to_all | solution.py:278
  37.1 1.2 %tile.9 = bf16[4,1152,128]{2,1,0:T(8,128)(2,1)} broadcast(bf16[1152,128]{1,0:T(8,128)(2,1)S(1)} %bitcast.12), dimensions={1,2} | broadcast | bytes 1474560 | tf_op jit(solution)/shard_map/tile | solution.py:279
  38.2 4.3 %all-to-all-start.1 = ((bf16[4,1152,128]{2,1,0:T(8,128)(2,1)}), bf16[4,1152,128]{2,1,0:T(8,128)(2,1)}, u32[]{:S(2)}, u32[]{:S(2)}) async-start(bf16[4,1152,128]{2,1,0:T(8,128)(2,1)} %tile.9), calls=%async_computation.1 | async-start | bytes 2359296 | tf_op jit(solution)/shard_map/all_to_all | solution.py:279
  42.5 0.0 copy-start.5
  42.5 0.0 copy-start
  42.5 2.2 %collective-permute-done.near_ref = bf16[256,2048]{1,0:T(8,128)(2,1)S(1)} collective-permute-done((bf16[256,2048]{1,0:T(8,128)(2,1)}, bf16[256,2048]{1,0:T(8,128)(2,1)S(1)}, u32[]{:S(2)}, u32[]{:S(2)}) %collective-permute-start) | collective-permute-done | bytes 1048608 | tf_op jit(solution)/shard_map/ppermute | solution.py:267
  44.8 4.9 %collective-permute-start.2 = (bf16[160,2048]{1,0:T(8,128)(2,1)S(1)}, bf16[160,2048]{1,0:T(8,128)(2,1)S(1)}, u32[]{:S(2)}, u32[]{:S(2)}) collective-permute-start(bf16[160,2048]{1,0:T(8,128)(2,1)S(1)} %slice.8), channel_id=1, source_target_pairs={{0,96},{32,64},{64,32},{96,0},{1,97},{33,65},{65,33},{97,1},{2,98}... | collective-permute-start | bytes 1966088 | tf_op jit(solution)/shard_map/ppermute | solution.py:267
  49.7 0.0 collective-permute-done.1.far_ref
  49.7 2.0 %collective-permute-start.3 = (bf16[96,2048]{1,0:T(8,128)(2,1)S(1)}, bf16[96,2048]{1,0:T(8,128)(2,1)S(1)}, u32[]{:S(2)}, u32[]{:S(2)}) collective-permute-start(bf16[96,2048]{1,0:T(8,128)(2,1)S(1)} %slice.9), channel_id=1, source_target_pairs={{0,32},{32,0},{64,96},{96,64},{1,33},{33,1},{65,97},{97,65},{2,34}... | collective-permute-start | bytes 1179656 | tf_op jit(solution)/shard_map/ppermute | solution.py:267
  51.8 8.9 %collective-permute-done.3.tail_ref = bf16[96,2048]{1,0:T(8,128)(2,1)S(1)} collective-permute-done((bf16[96,2048]{1,0:T(8,128)(2,1)S(1)}, bf16[96,2048]{1,0:T(8,128)(2,1)S(1)}, u32[]{:S(2)}, u32[]{:S(2)}) %collective-permute-start.3) | collective-permute-done | bytes 393248 | tf_op jit(solution)/shard_map/ppermute | solution.py:267
  60.7 2.5 %collective-permute-done.2.head_ref = bf16[160,2048]{1,0:T(8,128)(2,1)S(1)} collective-permute-done((bf16[160,2048]{1,0:T(8,128)(2,1)S(1)}, bf16[160,2048]{1,0:T(8,128)(2,1)S(1)}, u32[]{:S(2)}, u32[]{:S(2)}) %collective-permute-start.2) | collective-permute-done | bytes 655392 | tf_op jit(solution)/shard_map/ppermute | solution.py:267
  63.2 0.0 copy-start.1
  63.2 0.8 copy-done.1
  64.0 0.0 all-to-all-done.1
  64.0 1.9 %collective-permute-start.4 = (bf16[4608,128]{1,0:T(8,128)(2,1)}, bf16[4608,128]{1,0:T(8,128)(2,1)}, u32[]{:S(2)}, u32[]{:S(2)}) collective-permute-start(bf16[4608,128]{1,0:T(8,128)(2,1)} %bitcast.6), channel_id=1, source_target_pairs={{0,1},{1,0},{2,3},{3,2},{4,5},{5,4},{6,7},{7,6},{8,9},{9,8},{10,11... | collective-permute-start | bytes 3538952 | tf_op jit(solution)/shard_map/ppermute | solution.py:281
  66.6 0.0 copy-done.5
  66.6 0.6 dynamic_slice.3.bias
  67.3 0.1 pad_add_fusion.info
  67.3 1.8 %collective-permute-done.4 = bf16[4608,128]{1,0:T(8,128)(2,1)} collective-permute-done((bf16[4608,128]{1,0:T(8,128)(2,1)}, bf16[4608,128]{1,0:T(8,128)(2,1)}, u32[]{:S(2)}, u32[]{:S(2)}) %collective-permute-start.4) | collective-permute-done | bytes 1179680 | tf_op jit(solution)/shard_map/ppermute | solution.py:281
  69.1 0.0 copy-done
  69.1 0.0 copy-start.2
  69.1 1.1 %copy-done.2 = bf16[160,2048]{1,0:T(8,128)(2,1)S(1)} copy-done((bf16[160,2048]{1,0:T(8,128)(2,1)S(1)}, bf16[160,2048]{1,0:T(8,128)(2,1)}, u32[]{:S(2)}) %copy-start.2) | copy-done | bytes 655384
  70.2 6.9 %project.1 = (bf16[1024,128]{1,0:T(8,128)(2,1)S(1)}, bf16[128,1024]{1,0:T(8,128)(2,1)S(1)}, bf16[1024,256]{1,0:T(8,128)(2,1)S(1)}, f32[8,1024]{1,0:T(8,128)S(1)}, bf16[4,128,384]{2,1,0:T(8,128)(2,1)S(1)}) custom-call(s32[4]{0:T(128)S(1)} %pad_add_fusion.info, f32[1]{0:T(128)} %dynamic_slice.3.bias, bf16[1,256,2048]{2,1,0:T(8,128)(2,1)S(1)} %copy-done, ...), custom_call_target="tpu_custom_call" | custom-call | tf_op jit(solution)/shard_map/project/pallas_call | solution.py:189
  77.1 12.5 %all_to_all.20.states_ref = bf16[4,128,384]{2,1,0:T(8,128)(2,1)S(1)} all-to-all(bf16[4,128,384]{2,1,0:T(8,128)(2,1)S(1)} %get-tuple-element.20), channel_id=1, replica_groups=mesh['x'=4,'y'=4,'z'=16,'c'=2] {'x'}, dimensions={0} | all-to-all | bytes 786432 | tf_op jit(solution)/shard_map/all_to_all | solution.py:287
  89.6 2.7 %cell.1 = bf16[4,256,256]{2,1,0:T(8,128)(2,1)S(1)} custom-call(s32[4]{0:T(128)S(1)} %pad_add_fusion.info, bf16[1024,128]{1,0:T(8,128)(2,1)S(1)} %get-tuple-element.16.q_ref, bf16[128,1024]{1,0:T(8,128)(2,1)S(1)} %get-tuple-element.17.kt_ref, bf16[1024,256]{1,0:T(8,128)(2,1)S(1)} %get-tuple-element.18.v_ref, f32[8,1024]{1,0:T(8,128)S(1)} %get-tuple-element.19.rows_ref, ...), custom_call_target="tpu_custom_call" | custom-call | tf_op jit(solution)/shard_map/cell/pallas_call | solution.py:212
  92.3 12.1 %all_to_all.21.heads_ref = bf16[4,256,256]{2,1,0:T(8,128)(2,1)S(1)} all-to-all(bf16[4,256,256]{2,1,0:T(8,128)(2,1)S(1)} %cell.1), channel_id=1, replica_groups=mesh['x'=4,'y'=4,'z'=16,'c'=2] {'y'}, dimensions={0} | all-to-all | bytes 1048576 | tf_op jit(solution)/shard_map/all_to_all | solution.py:289
  104.4 0.9 merge.1
  (2 shorter events, 0.1 us)
Async XLA Ops:
  0.1 0.9 copy-start.3
  1.0 0.7 copy-start.4
  3.1 34.0 %all-to-all-start = ((bf16[16,72,128]{2,1,0:T(8,128)(2,1)}), bf16[16,72,128]{2,1,0:T(8,128)(2,1)S(1)}, u32[]{:S(2)}, u32[]{:S(2)}) async-start(bf16[16,72,128]{2,1,0:T(8,128)(2,1)} %piece.1), calls=%async_computation | async-start | bytes 589824 | tf_op jit(solution)/shard_map/all_to_all | solution.py:278
  18.3 26.4 %collective-permute-start = (bf16[256,2048]{1,0:T(8,128)(2,1)}, bf16[256,2048]{1,0:T(8,128)(2,1)S(1)}, u32[]{:S(2)}, u32[]{:S(2)}) collective-permute-start(bf16[256,2048]{1,0:T(8,128)(2,1)} %bitcast.9), channel_id=1, source_target_pairs={{0,32},{32,0},{64,96},{96,64},{1,33},{33,1},{65,97},{97,65},{2,34}... | collective-permute-start | bytes 3145736 | tf_op jit(solution)/shard_map/ppermute | solution.py:267
  21.8 27.9 %collective-permute-start.1 = (bf16[256,2048]{1,0:T(8,128)(2,1)}, bf16[256,2048]{1,0:T(8,128)(2,1)S(1)}, u32[]{:S(2)}, u32[]{:S(2)}) collective-permute-start(bf16[256,2048]{1,0:T(8,128)(2,1)} %bitcast.10), channel_id=1, source_target_pairs={{0,96},{32,64},{64,32},{96,0},{1,97},{33,65},{65,33},{97,1},{2,98}... | collective-permute-start | bytes 3145736 | tf_op jit(solution)/shard_map/ppermute | solution.py:267
  38.2 25.8 %all-to-all-start.1 = ((bf16[4,1152,128]{2,1,0:T(8,128)(2,1)}), bf16[4,1152,128]{2,1,0:T(8,128)(2,1)}, u32[]{:S(2)}, u32[]{:S(2)}) async-start(bf16[4,1152,128]{2,1,0:T(8,128)(2,1)} %tile.9), calls=%async_computation.1 | async-start | bytes 2359296 | tf_op jit(solution)/shard_map/all_to_all | solution.py:279
  42.5 24.1 %copy-start.5 = (f32[4]{0:T(128)S(1)}, f32[4]{0:T(128)}, u32[]{:S(2)}) copy-start(f32[4]{0:T(128)} %param.8) | copy-start | bytes 52
  42.5 26.6 %copy-start = (bf16[1,256,2048]{2,1,0:T(8,128)(2,1)S(1)}, bf16[1,256,2048]{2,1,0:T(8,128)(2,1)}, u32[]{:S(2)}) copy-start(bf16[1,256,2048]{2,1,0:T(8,128)(2,1)} %x_ref.1) | copy-start | bytes 3145732
  44.8 18.4 %collective-permute-start.2 = (bf16[160,2048]{1,0:T(8,128)(2,1)S(1)}, bf16[160,2048]{1,0:T(8,128)(2,1)S(1)}, u32[]{:S(2)}, u32[]{:S(2)}) collective-permute-start(bf16[160,2048]{1,0:T(8,128)(2,1)S(1)} %slice.8), channel_id=1, source_target_pairs={{0,96},{32,64},{64,32},{96,0},{1,97},{33,65},{65,33},{97,1},{2,98}... | collective-permute-start | bytes 1966088 | tf_op jit(solution)/shard_map/ppermute | solution.py:267
  49.7 11.0 %collective-permute-start.3 = (bf16[96,2048]{1,0:T(8,128)(2,1)S(1)}, bf16[96,2048]{1,0:T(8,128)(2,1)S(1)}, u32[]{:S(2)}, u32[]{:S(2)}) collective-permute-start(bf16[96,2048]{1,0:T(8,128)(2,1)S(1)} %slice.9), channel_id=1, source_target_pairs={{0,32},{32,0},{64,96},{96,64},{1,33},{33,1},{65,97},{97,65},{2,34}... | collective-permute-start | bytes 1179656 | tf_op jit(solution)/shard_map/ppermute | solution.py:267
  63.2 0.8 copy-start.1
  64.0 5.1 %collective-permute-start.4 = (bf16[4608,128]{1,0:T(8,128)(2,1)}, bf16[4608,128]{1,0:T(8,128)(2,1)}, u32[]{:S(2)}, u32[]{:S(2)}) collective-permute-start(bf16[4608,128]{1,0:T(8,128)(2,1)} %bitcast.6), channel_id=1, source_target_pairs={{0,1},{1,0},{2,3},{3,2},{4,5},{5,4},{6,7},{7,6},{8,9},{9,8},{10,11... | collective-permute-start | bytes 3538952 | tf_op jit(solution)/shard_map/ppermute | solution.py:281
  69.1 1.1 %copy-start.2 = (bf16[160,2048]{1,0:T(8,128)(2,1)S(1)}, bf16[160,2048]{1,0:T(8,128)(2,1)}, u32[]{:S(2)}) copy-start(bf16[160,2048]{1,0:T(8,128)(2,1)} %copy-done.1) | copy-start | bytes 1966084

commit v7 on v6

--- a/solution.py
+++ b/solution.py
@@ -14,7 +14,7 @@
 NX, NY, NZ, NC = 4, 4, 16, 2
 QUAD = NY * TOK
 HALF = D // (NZ * NC)
-CUT = 160
+CUT = 144
 PIECE = HALF + 8
 EXT = DV + 128
 WIDE = 2 * DK + DV + 128
@@ -202,7 +202,7 @@
             pltpu.VMEM((8, QUAD), jnp.float32),
             pltpu.VMEM((8, QUAD), jnp.float32),
         ],
-        compiler_params=granted(48),
+        compiler_params=granted(49),
         name="project",
         **options,
     )(info, bias, *tokens, own, other)

time: 106 us -> 103 us (0.972)
  blocking collectives: 24.6 us -> 23.5 us
    unnamed x12 -> x8, local copies, waits for them, and re-layouts: 3.57 us -> 1.64 us
    all_to_all x1, blocking collectives: 12.1 us -> 11 us  [per_device(): return merge(lax.all_to_all(out, 'y', 0, 0, tiled=True))]
  transfers between devices with their start and end apart: 7 -> 7, of which waited for: 5 -> 4; matrix products, arithmetic and copies ran while one was open for 2% -> 3% of each run, Pallas kernels for 0% -> 0%
where the time goes in v7:
time: 103 us
  starting transfers between devices  36 us (35%)
  waiting for transfers between devices  25.7 us (25%)
  blocking collectives  23.5 us (23%)
  Pallas kernels  12 us (12%)
  local copies, waits for them, and re-layouts  4.49 us (4%)
    all_to_all x1, starting transfers between devices, per_device(): lax.all_to_all(weight_piece(place, proj_weight, gate_weight), 'z', 0, 0)  15.2 us
    ppermute x4, starting transfers between devices, swap_along(): return lax.ppermute(array, axis, [(i, i ^ swap) for i in range(4)])  14.5 us
    ppermute x4, waiting for transfers between devices, swap_along(): return lax.ppermute(array, axis, [(i, i ^ swap) for i in range(4)])  12.6 us
    all_to_all x1, blocking collectives, per_device(): states = lax.all_to_all(sent, 'x', 0, 0, tiled=True)  12.5 us
    all_to_all x1, waiting for transfers between devices, per_device(): lax.all_to_all(weight_piece(place, proj_weight, gate_weight), 'z', 0, 0)  11.2 us
    all_to_all x1, blocking collectives, per_device(): return merge(lax.all_to_all(out, 'y', 0, 0, tiled=True))  11 us
    pallas_call x1, Pallas kernels, project(): pl.pallas_call(project_kernel, out_shape=(shaped(QUAD, DK), shaped(DK, QU...  7.16 us
    all_to_all x1, starting transfers between devices, per_device(): lax.all_to_all(jnp.tile(rows.reshape(1, NZ * PIECE, 128), (NX, 1, 1)), 'x...  4.29 us
  transfers between devices with their start and end apart: 7, of which 4 were waited for; matrix products, arithmetic and copies ran while one was open for 3% of the time, Pallas kernels for 0%

profile of v7, /device:TPU:32, one launch (start us, length us, event | category | flops | bytes accessed | tf_op | source)
XLA Modules:
  0.0 102.5 jit_solution(8921974344530327963)
XLA Ops:
  0.0 0.1 pad_add_fusion.1.place
  0.1 0.0 copy-start.1
  0.1 0.9 copy-done.1
  1.0 0.0 copy-start.2
  1.0 0.7 copy-done.2
  1.7 1.4 %piece.1 = bf16[16,72,128]{2,1,0:T(8,128)(2,1)} custom-call(s32[2]{0:T(128)S(1)} %pad_add_fusion.1.place, bf16[64,2048]{1,0:T(8,128)(2,1)S(1)} %copy-done.1, bf16[8,64]{1,0:T(8,128)(2,1)S(1)} %bitcast.11), custom_call_target="tpu_custom_call" | custom-call | tf_op jit(solution)/shard_map/piece/pallas_call | solution.py:255
  3.1 15.2 %all-to-all-start = ((bf16[16,72,128]{2,1,0:T(8,128)(2,1)}), bf16[16,72,128]{2,1,0:T(8,128)(2,1)S(1)}, u32[]{:S(2)}, u32[]{:S(2)}) async-start(bf16[16,72,128]{2,1,0:T(8,128)(2,1)} %piece.1), calls=%async_computation | async-start | bytes 589824 | tf_op jit(solution)/shard_map/all_to_all | solution.py:278
  18.3 3.5 %collective-permute-start = (bf16[256,2048]{1,0:T(8,128)(2,1)}, bf16[256,2048]{1,0:T(8,128)(2,1)S(1)}, u32[]{:S(2)}, u32[]{:S(2)}) collective-permute-start(bf16[256,2048]{1,0:T(8,128)(2,1)} %bitcast.9), channel_id=1, source_target_pairs={{0,32},{32,0},{64,96},{96,64},{1,33},{33,1},{65,97},{97,65},{2,34}... | collective-permute-start | bytes 3145736 | tf_op jit(solution)/shard_map/ppermute | solution.py:267
  21.8 4.1 %collective-permute-start.1 = (bf16[256,2048]{1,0:T(8,128)(2,1)}, bf16[256,2048]{1,0:T(8,128)(2,1)}, u32[]{:S(2)}, u32[]{:S(2)}) collective-permute-start(bf16[256,2048]{1,0:T(8,128)(2,1)} %bitcast.10), channel_id=1, source_target_pairs={{0,96},{32,64},{64,32},{96,0},{1,97},{33,65},{65,33},{97,1},{2,98}... | collective-permute-start | bytes 3145736 | tf_op jit(solution)/shard_map/ppermute | solution.py:267
  25.9 11.2 %all-to-all-done = bf16[16,72,128]{2,1,0:T(8,128)(2,1)S(1)} async-done(((bf16[16,72,128]{2,1,0:T(8,128)(2,1)}), bf16[16,72,128]{2,1,0:T(8,128)(2,1)S(1)}, u32[]{:S(2)}, u32[]{:S(2)}) %all-to-all-start) | async-done | bytes 294944 | tf_op jit(solution)/shard_map/all_to_all | solution.py:278
  37.1 1.2 %tile.9 = bf16[4,1152,128]{2,1,0:T(8,128)(2,1)} broadcast(bf16[1152,128]{1,0:T(8,128)(2,1)S(1)} %bitcast.12), dimensions={1,2} | broadcast | bytes 1474560 | tf_op jit(solution)/shard_map/tile | solution.py:279
  38.2 4.3 %all-to-all-start.1 = ((bf16[4,1152,128]{2,1,0:T(8,128)(2,1)}), bf16[4,1152,128]{2,1,0:T(8,128)(2,1)}, u32[]{:S(2)}, u32[]{:S(2)}) async-start(bf16[4,1152,128]{2,1,0:T(8,128)(2,1)} %tile.9), calls=%async_computation.1 | async-start | bytes 2359296 | tf_op jit(solution)/shard_map/all_to_all | solution.py:279
  42.5 0.0 copy-start.3
  42.5 0.0 copy-start
  42.5 2.2 %collective-permute-done.near_ref = bf16[256,2048]{1,0:T(8,128)(2,1)S(1)} collective-permute-done((bf16[256,2048]{1,0:T(8,128)(2,1)}, bf16[256,2048]{1,0:T(8,128)(2,1)S(1)}, u32[]{:S(2)}, u32[]{:S(2)}) %collective-permute-start) | collective-permute-done | bytes 1048608 | tf_op jit(solution)/shard_map/ppermute | solution.py:267
  44.8 4.9 %collective-permute-start.2 = (bf16[144,2048]{1,0:T(8,128)(2,1)S(1)}, bf16[144,2048]{1,0:T(8,128)(2,1)S(1)}, u32[]{:S(2)}, u32[]{:S(2)}) collective-permute-start(bf16[144,2048]{1,0:T(8,128)(2,1)S(1)} %slice.8), channel_id=1, source_target_pairs={{0,96},{32,64},{64,32},{96,0},{1,97},{33,65},{65,33},{97,1},{2,98}... | collective-permute-start | bytes 1769480 | tf_op jit(solution)/shard_map/ppermute | solution.py:267
  49.7 0.0 collective-permute-done.1.far_ref
  49.7 1.1 %slice.9 = bf16[112,2048]{1,0:T(8,128)(2,1)S(1)} slice(bf16[256,2048]{1,0:T(8,128)(2,1)} %collective-permute-done.1.far_ref), slice={[144:256], [0:2048]} | slice | bytes 917504 | tf_op jit(solution)/shard_map/slice | solution.py:276
  50.8 2.0 %collective-permute-start.3 = (bf16[112,2048]{1,0:T(8,128)(2,1)S(1)}, bf16[112,2048]{1,0:T(8,128)(2,1)S(1)}, u32[]{:S(2)}, u32[]{:S(2)}) collective-permute-start(bf16[112,2048]{1,0:T(8,128)(2,1)S(1)} %slice.9), channel_id=1, source_target_pairs={{0,32},{32,0},{64,96},{96,64},{1,33},{33,1},{65,97},{97,65},{2,34}... | collective-permute-start | bytes 1376264 | tf_op jit(solution)/shard_map/ppermute | solution.py:267
  52.8 10.4 %collective-permute-done.3.tail_ref = bf16[112,2048]{1,0:T(8,128)(2,1)S(1)} collective-permute-done((bf16[112,2048]{1,0:T(8,128)(2,1)S(1)}, bf16[112,2048]{1,0:T(8,128)(2,1)S(1)}, u32[]{:S(2)}, u32[]{:S(2)}) %collective-permute-start.3) | collective-permute-done | bytes 458784 | tf_op jit(solution)/shard_map/ppermute | solution.py:267
  63.3 0.0 collective-permute-done.2.head_ref
  63.3 0.0 all-to-all-done.1
  63.3 1.9 %collective-permute-start.4 = (bf16[4608,128]{1,0:T(8,128)(2,1)}, bf16[4608,128]{1,0:T(8,128)(2,1)}, u32[]{:S(2)}, u32[]{:S(2)}) collective-permute-start(bf16[4608,128]{1,0:T(8,128)(2,1)} %bitcast.6), channel_id=1, source_target_pairs={{0,1},{1,0},{2,3},{3,2},{4,5},{5,4},{6,7},{7,6},{8,9},{9,8},{10,11... | collective-permute-start | bytes 3538952 | tf_op jit(solution)/shard_map/ppermute | solution.py:281
  65.8 0.0 copy-done.3
  65.8 0.6 dynamic_slice.3.bias
  66.4 0.1 pad_add_fusion.info
  66.5 1.8 %collective-permute-done.4 = bf16[4608,128]{1,0:T(8,128)(2,1)} collective-permute-done((bf16[4608,128]{1,0:T(8,128)(2,1)}, bf16[4608,128]{1,0:T(8,128)(2,1)}, u32[]{:S(2)}, u32[]{:S(2)}) %collective-permute-start.4) | collective-permute-done | bytes 1179680 | tf_op jit(solution)/shard_map/ppermute | solution.py:281
  68.3 0.0 copy-done
  68.3 7.2 %project.1 = (bf16[1024,128]{1,0:T(8,128)(2,1)S(1)}, bf16[128,1024]{1,0:T(8,128)(2,1)S(1)}, bf16[1024,256]{1,0:T(8,128)(2,1)S(1)}, f32[8,1024]{1,0:T(8,128)S(1)}, bf16[4,128,384]{2,1,0:T(8,128)(2,1)S(1)}) custom-call(s32[4]{0:T(128)S(1)} %pad_add_fusion.info, f32[1]{0:T(128)} %dynamic_slice.3.bias, bf16[1,256,2048]{2,1,0:T(8,128)(2,1)S(1)} %copy-done, ...), custom_call_target="tpu_custom_call" | custom-call | tf_op jit(solution)/shard_map/project/pallas_call | solution.py:189
  75.5 12.5 %all_to_all.20.states_ref = bf16[4,128,384]{2,1,0:T(8,128)(2,1)S(1)} all-to-all(bf16[4,128,384]{2,1,0:T(8,128)(2,1)S(1)} %get-tuple-element.20), channel_id=1, replica_groups=mesh['x'=4,'y'=4,'z'=16,'c'=2] {'x'}, dimensions={0} | all-to-all | bytes 786432 | tf_op jit(solution)/shard_map/all_to_all | solution.py:287
  88.0 2.7 %cell.1 = bf16[4,256,256]{2,1,0:T(8,128)(2,1)S(1)} custom-call(s32[4]{0:T(128)S(1)} %pad_add_fusion.info, bf16[1024,128]{1,0:T(8,128)(2,1)S(1)} %get-tuple-element.16.q_ref, bf16[128,1024]{1,0:T(8,128)(2,1)S(1)} %get-tuple-element.17.kt_ref, bf16[1024,256]{1,0:T(8,128)(2,1)S(1)} %get-tuple-element.18.v_ref, f32[8,1024]{1,0:T(8,128)S(1)} %get-tuple-element.19.rows_ref, ...), custom_call_target="tpu_custom_call" | custom-call | tf_op jit(solution)/shard_map/cell/pallas_call | solution.py:212
  90.6 11.0 %all_to_all.21.heads_ref = bf16[4,256,256]{2,1,0:T(8,128)(2,1)S(1)} all-to-all(bf16[4,256,256]{2,1,0:T(8,128)(2,1)S(1)} %cell.1), channel_id=1, replica_groups=mesh['x'=4,'y'=4,'z'=16,'c'=2] {'y'}, dimensions={0} | all-to-all | bytes 1048576 | tf_op jit(solution)/shard_map/all_to_all | solution.py:289
  101.7 0.9 merge.1
  (1 shorter events, 0.0 us)
Async XLA Ops:
  0.1 0.9 copy-start.1
  1.0 0.7 copy-start.2
  3.1 34.0 %all-to-all-start = ((bf16[16,72,128]{2,1,0:T(8,128)(2,1)}), bf16[16,72,128]{2,1,0:T(8,128)(2,1)S(1)}, u32[]{:S(2)}, u32[]{:S(2)}) async-start(bf16[16,72,128]{2,1,0:T(8,128)(2,1)} %piece.1), calls=%async_computation | async-start | bytes 589824 | tf_op jit(solution)/shard_map/all_to_all | solution.py:278
  18.3 26.4 %collective-permute-start = (bf16[256,2048]{1,0:T(8,128)(2,1)}, bf16[256,2048]{1,0:T(8,128)(2,1)S(1)}, u32[]{:S(2)}, u32[]{:S(2)}) collective-permute-start(bf16[256,2048]{1,0:T(8,128)(2,1)} %bitcast.9), channel_id=1, source_target_pairs={{0,32},{32,0},{64,96},{96,64},{1,33},{33,1},{65,97},{97,65},{2,34}... | collective-permute-start | bytes 3145736 | tf_op jit(solution)/shard_map/ppermute | solution.py:267
  21.8 27.9 %collective-permute-start.1 = (bf16[256,2048]{1,0:T(8,128)(2,1)}, bf16[256,2048]{1,0:T(8,128)(2,1)}, u32[]{:S(2)}, u32[]{:S(2)}) collective-permute-start(bf16[256,2048]{1,0:T(8,128)(2,1)} %bitcast.10), channel_id=1, source_target_pairs={{0,96},{32,64},{64,32},{96,0},{1,97},{33,65},{65,33},{97,1},{2,98}... | collective-permute-start | bytes 3145736 | tf_op jit(solution)/shard_map/ppermute | solution.py:267
  38.2 25.0 %all-to-all-start.1 = ((bf16[4,1152,128]{2,1,0:T(8,128)(2,1)}), bf16[4,1152,128]{2,1,0:T(8,128)(2,1)}, u32[]{:S(2)}, u32[]{:S(2)}) async-start(bf16[4,1152,128]{2,1,0:T(8,128)(2,1)} %tile.9), calls=%async_computation.1 | async-start | bytes 2359296 | tf_op jit(solution)/shard_map/all_to_all | solution.py:279
  42.5 23.3 %copy-start.3 = (f32[4]{0:T(128)S(1)}, f32[4]{0:T(128)}, u32[]{:S(2)}) copy-start(f32[4]{0:T(128)} %param.8) | copy-start | bytes 52
  42.5 25.8 %copy-start = (bf16[1,256,2048]{2,1,0:T(8,128)(2,1)S(1)}, bf16[1,256,2048]{2,1,0:T(8,128)(2,1)}, u32[]{:S(2)}) copy-start(bf16[1,256,2048]{2,1,0:T(8,128)(2,1)} %x_ref.1) | copy-start | bytes 3145732
  44.8 18.5 %collective-permute-start.2 = (bf16[144,2048]{1,0:T(8,128)(2,1)S(1)}, bf16[144,2048]{1,0:T(8,128)(2,1)S(1)}, u32[]{:S(2)}, u32[]{:S(2)}) collective-permute-start(bf16[144,2048]{1,0:T(8,128)(2,1)S(1)} %slice.8), channel_id=1, source_target_pairs={{0,96},{32,64},{64,32},{96,0},{1,97},{33,65},{65,33},{97,1},{2,98}... | collective-permute-start | bytes 1769480 | tf_op jit(solution)/shard_map/ppermute | solution.py:267
  50.8 12.5 %collective-permute-start.3 = (bf16[112,2048]{1,0:T(8,128)(2,1)S(1)}, bf16[112,2048]{1,0:T(8,128)(2,1)S(1)}, u32[]{:S(2)}, u32[]{:S(2)}) collective-permute-start(bf16[112,2048]{1,0:T(8,128)(2,1)S(1)} %slice.9), channel_id=1, source_target_pairs={{0,32},{32,0},{64,96},{96,64},{1,33},{33,1},{65,97},{97,65},{2,34}... | collective-permute-start | bytes 1376264 | tf_op jit(solution)/shard_map/ppermute | solution.py:267
  63.3 5.1 %collective-permute-start.4 = (bf16[4608,128]{1,0:T(8,128)(2,1)}, bf16[4608,128]{1,0:T(8,128)(2,1)}, u32[]{:S(2)}, u32[]{:S(2)}) collective-permute-start(bf16[4608,128]{1,0:T(8,128)(2,1)} %bitcast.6), channel_id=1, source_target_pairs={{0,1},{1,0},{2,3},{3,2},{4,5},{5,4},{6,7},{7,6},{8,9},{9,8},{10,11... | collective-permute-start | bytes 3538952 | tf_op jit(solution)/shard_map/ppermute | solution.py:281

commit v8 on v7

--- a/solution.py
+++ b/solution.py
@@ -14,7 +14,7 @@
 NX, NY, NZ, NC = 4, 4, 16, 2
 QUAD = NY * TOK
 HALF = D // (NZ * NC)
-CUT = 144
+CUT = 160
 PIECE = HALF + 8
 EXT = DV + 128
 WIDE = 2 * DK + DV + 128

time: 103 us -> 104 us (level)
  blocking collectives: 23.5 us -> 24.7 us
    all_to_all x1, blocking collectives: 11 us -> 12.2 us  [per_device(): return merge(lax.all_to_all(out, 'y', 0, 0, tiled=True))]
  transfers between devices with their start and end apart: 7 -> 7, of which waited for: 4 -> 5; matrix products, arithmetic and copies ran while one was open for 3% -> 3% of each run, Pallas kernels for 0% -> 0%
where the time goes in v8:
time: 104 us
  starting transfers between devices  36 us (35%)
  waiting for transfers between devices  25.6 us (25%)
  blocking collectives  24.7 us (24%)
  Pallas kernels  12 us (12%)
  local copies, waits for them, and re-layouts  4.46 us (4%)
    all_to_all x1, starting transfers between devices, per_device(): lax.all_to_all(weight_piece(place, proj_weight, gate_weight), 'z', 0, 0)  15.2 us
    ppermute x4, starting transfers between devices, swap_along(): return lax.ppermute(array, axis, [(i, i ^ swap) for i in range(4)])  14.5 us
    ppermute x4, waiting for transfers between devices, swap_along(): return lax.ppermute(array, axis, [(i, i ^ swap) for i in range(4)])  12.6 us
    all_to_all x1, blocking collectives, per_device(): states = lax.all_to_all(sent, 'x', 0, 0, tiled=True)  12.5 us
    all_to_all x1, blocking collectives, per_device(): return merge(lax.all_to_all(out, 'y', 0, 0, tiled=True))  12.2 us
    all_to_all x1, waiting for transfers between devices, per_device(): lax.all_to_all(weight_piece(place, proj_weight, gate_weight), 'z', 0, 0)  11.2 us
    pallas_call x1, Pallas kernels, project(): pl.pallas_call(project_kernel, out_shape=(shaped(QUAD, DK), shaped(DK, QU...  7.16 us
    all_to_all x1, starting transfers between devices, per_device(): lax.all_to_all(jnp.tile(rows.reshape(1, NZ * PIECE, 128), (NX, 1, 1)), 'x...  4.29 us
  transfers between devices with their start and end apart: 7, of which 5 were waited for; matrix products, arithmetic and copies ran while one was open for 3% of the time, Pallas kernels for 0%

profile of v8, /device:TPU:32, one launch (start us, length us, event | category | flops | bytes accessed | tf_op | source)
XLA Modules:
  0.0 103.6 jit_solution(11086376341395840162)
XLA Ops:
  0.0 0.1 pad_add_fusion.1.place
  0.1 0.0 copy-start.1
  0.1 0.9 copy-done.1
  1.0 0.0 copy-start.2
  1.0 0.7 copy-done.2
  1.7 1.4 %piece.1 = bf16[16,72,128]{2,1,0:T(8,128)(2,1)} custom-call(s32[2]{0:T(128)S(1)} %pad_add_fusion.1.place, bf16[64,2048]{1,0:T(8,128)(2,1)S(1)} %copy-done.1, bf16[8,64]{1,0:T(8,128)(2,1)S(1)} %bitcast.11), custom_call_target="tpu_custom_call" | custom-call | tf_op jit(solution)/shard_map/piece/pallas_call | solution.py:255
  3.1 15.2 %all-to-all-start = ((bf16[16,72,128]{2,1,0:T(8,128)(2,1)}), bf16[16,72,128]{2,1,0:T(8,128)(2,1)S(1)}, u32[]{:S(2)}, u32[]{:S(2)}) async-start(bf16[16,72,128]{2,1,0:T(8,128)(2,1)} %piece.1), calls=%async_computation | async-start | bytes 589824 | tf_op jit(solution)/shard_map/all_to_all | solution.py:278
  18.3 3.5 %collective-permute-start = (bf16[256,2048]{1,0:T(8,128)(2,1)}, bf16[256,2048]{1,0:T(8,128)(2,1)S(1)}, u32[]{:S(2)}, u32[]{:S(2)}) collective-permute-start(bf16[256,2048]{1,0:T(8,128)(2,1)} %bitcast.9), channel_id=1, source_target_pairs={{0,32},{32,0},{64,96},{96,64},{1,33},{33,1},{65,97},{97,65},{2,34}... | collective-permute-start | bytes 3145736 | tf_op jit(solution)/shard_map/ppermute | solution.py:267
  21.8 4.1 %collective-permute-start.1 = (bf16[256,2048]{1,0:T(8,128)(2,1)}, bf16[256,2048]{1,0:T(8,128)(2,1)}, u32[]{:S(2)}, u32[]{:S(2)}) collective-permute-start(bf16[256,2048]{1,0:T(8,128)(2,1)} %bitcast.10), channel_id=1, source_target_pairs={{0,96},{32,64},{64,32},{96,0},{1,97},{33,65},{65,33},{97,1},{2,98}... | collective-permute-start | bytes 3145736 | tf_op jit(solution)/shard_map/ppermute | solution.py:267
  25.9 11.2 %all-to-all-done = bf16[16,72,128]{2,1,0:T(8,128)(2,1)S(1)} async-done(((bf16[16,72,128]{2,1,0:T(8,128)(2,1)}), bf16[16,72,128]{2,1,0:T(8,128)(2,1)S(1)}, u32[]{:S(2)}, u32[]{:S(2)}) %all-to-all-start) | async-done | bytes 294944 | tf_op jit(solution)/shard_map/all_to_all | solution.py:278
  37.1 1.2 %tile.9 = bf16[4,1152,128]{2,1,0:T(8,128)(2,1)} broadcast(bf16[1152,128]{1,0:T(8,128)(2,1)S(1)} %bitcast.12), dimensions={1,2} | broadcast | bytes 1474560 | tf_op jit(solution)/shard_map/tile | solution.py:279
  38.2 4.3 %all-to-all-start.1 = ((bf16[4,1152,128]{2,1,0:T(8,128)(2,1)}), bf16[4,1152,128]{2,1,0:T(8,128)(2,1)}, u32[]{:S(2)}, u32[]{:S(2)}) async-start(bf16[4,1152,128]{2,1,0:T(8,128)(2,1)} %tile.9), calls=%async_computation.1 | async-start | bytes 2359296 | tf_op jit(solution)/shard_map/all_to_all | solution.py:279
  42.5 0.0 copy-start.3
  42.5 0.0 copy-start
  42.5 2.2 %collective-permute-done.near_ref = bf16[256,2048]{1,0:T(8,128)(2,1)S(1)} collective-permute-done((bf16[256,2048]{1,0:T(8,128)(2,1)}, bf16[256,2048]{1,0:T(8,128)(2,1)S(1)}, u32[]{:S(2)}, u32[]{:S(2)}) %collective-permute-start) | collective-permute-done | bytes 1048608 | tf_op jit(solution)/shard_map/ppermute | solution.py:267
  44.8 4.9 %collective-permute-start.2 = (bf16[160,2048]{1,0:T(8,128)(2,1)S(1)}, bf16[160,2048]{1,0:T(8,128)(2,1)S(1)}, u32[]{:S(2)}, u32[]{:S(2)}) collective-permute-start(bf16[160,2048]{1,0:T(8,128)(2,1)S(1)} %slice.8), channel_id=1, source_target_pairs={{0,96},{32,64},{64,32},{96,0},{1,97},{33,65},{65,33},{97,1},{2,98}... | collective-permute-start | bytes 1966088 | tf_op jit(solution)/shard_map/ppermute | solution.py:267
  49.7 0.0 collective-permute-done.1.far_ref
  49.7 1.0 slice.9
  50.7 2.0 %collective-permute-start.3 = (bf16[96,2048]{1,0:T(8,128)(2,1)S(1)}, bf16[96,2048]{1,0:T(8,128)(2,1)S(1)}, u32[]{:S(2)}, u32[]{:S(2)}) collective-permute-start(bf16[96,2048]{1,0:T(8,128)(2,1)S(1)} %slice.9), channel_id=1, source_target_pairs={{0,32},{32,0},{64,96},{96,64},{1,33},{33,1},{65,97},{97,65},{2,34}... | collective-permute-start | bytes 1179656 | tf_op jit(solution)/shard_map/ppermute | solution.py:267
  52.8 9.0 %collective-permute-done.3.tail_ref = bf16[96,2048]{1,0:T(8,128)(2,1)S(1)} collective-permute-done((bf16[96,2048]{1,0:T(8,128)(2,1)S(1)}, bf16[96,2048]{1,0:T(8,128)(2,1)S(1)}, u32[]{:S(2)}, u32[]{:S(2)}) %collective-permute-start.3) | collective-permute-done | bytes 393248 | tf_op jit(solution)/shard_map/ppermute | solution.py:267
  61.8 1.4 %collective-permute-done.2.head_ref = bf16[160,2048]{1,0:T(8,128)(2,1)S(1)} collective-permute-done((bf16[160,2048]{1,0:T(8,128)(2,1)S(1)}, bf16[160,2048]{1,0:T(8,128)(2,1)S(1)}, u32[]{:S(2)}, u32[]{:S(2)}) %collective-permute-start.2) | collective-permute-done | bytes 655392 | tf_op jit(solution)/shard_map/ppermute | solution.py:267
  63.2 0.0 all-to-all-done.1
  63.2 1.9 %collective-permute-start.4 = (bf16[4608,128]{1,0:T(8,128)(2,1)}, bf16[4608,128]{1,0:T(8,128)(2,1)}, u32[]{:S(2)}, u32[]{:S(2)}) collective-permute-start(bf16[4608,128]{1,0:T(8,128)(2,1)} %bitcast.6), channel_id=1, source_target_pairs={{0,1},{1,0},{2,3},{3,2},{4,5},{5,4},{6,7},{7,6},{8,9},{9,8},{10,11... | collective-permute-start | bytes 3538952 | tf_op jit(solution)/shard_map/ppermute | solution.py:281
  65.8 0.0 copy-done.3
  65.8 0.6 dynamic_slice.3.bias
  66.4 0.1 pad_add_fusion.info
  66.4 1.8 %collective-permute-done.4 = bf16[4608,128]{1,0:T(8,128)(2,1)} collective-permute-done((bf16[4608,128]{1,0:T(8,128)(2,1)}, bf16[4608,128]{1,0:T(8,128)(2,1)}, u32[]{:S(2)}, u32[]{:S(2)}) %collective-permute-start.4) | collective-permute-done | bytes 1179680 | tf_op jit(solution)/shard_map/ppermute | solution.py:281
  68.3 0.0 copy-done
  68.3 7.2 %project.1 = (bf16[1024,128]{1,0:T(8,128)(2,1)S(1)}, bf16[128,1024]{1,0:T(8,128)(2,1)S(1)}, bf16[1024,256]{1,0:T(8,128)(2,1)S(1)}, f32[8,1024]{1,0:T(8,128)S(1)}, bf16[4,128,384]{2,1,0:T(8,128)(2,1)S(1)}) custom-call(s32[4]{0:T(128)S(1)} %pad_add_fusion.info, f32[1]{0:T(128)} %dynamic_slice.3.bias, bf16[1,256,2048]{2,1,0:T(8,128)(2,1)S(1)} %copy-done, ...), custom_call_target="tpu_custom_call" | custom-call | tf_op jit(solution)/shard_map/project/pallas_call | solution.py:189
  75.4 12.5 %all_to_all.20.states_ref = bf16[4,128,384]{2,1,0:T(8,128)(2,1)S(1)} all-to-all(bf16[4,128,384]{2,1,0:T(8,128)(2,1)S(1)} %get-tuple-element.20), channel_id=1, replica_groups=mesh['x'=4,'y'=4,'z'=16,'c'=2] {'x'}, dimensions={0} | all-to-all | bytes 786432 | tf_op jit(solution)/shard_map/all_to_all | solution.py:287
  87.9 2.7 %cell.1 = bf16[4,256,256]{2,1,0:T(8,128)(2,1)S(1)} custom-call(s32[4]{0:T(128)S(1)} %pad_add_fusion.info, bf16[1024,128]{1,0:T(8,128)(2,1)S(1)} %get-tuple-element.16.q_ref, bf16[128,1024]{1,0:T(8,128)(2,1)S(1)} %get-tuple-element.17.kt_ref, bf16[1024,256]{1,0:T(8,128)(2,1)S(1)} %get-tuple-element.18.v_ref, f32[8,1024]{1,0:T(8,128)S(1)} %get-tuple-element.19.rows_ref, ...), custom_call_target="tpu_custom_call" | custom-call | tf_op jit(solution)/shard_map/cell/pallas_call | solution.py:212
  90.6 12.2 %all_to_all.21.heads_ref = bf16[4,256,256]{2,1,0:T(8,128)(2,1)S(1)} all-to-all(bf16[4,256,256]{2,1,0:T(8,128)(2,1)S(1)} %cell.1), channel_id=1, replica_groups=mesh['x'=4,'y'=4,'z'=16,'c'=2] {'y'}, dimensions={0} | all-to-all | bytes 1048576 | tf_op jit(solution)/shard_map/all_to_all | solution.py:289
  102.8 0.9 merge.1
  (1 shorter events, 0.0 us)
Async XLA Ops:
  0.1 0.9 copy-start.1
  1.0 0.7 copy-start.2
  3.1 34.0 %all-to-all-start = ((bf16[16,72,128]{2,1,0:T(8,128)(2,1)}), bf16[16,72,128]{2,1,0:T(8,128)(2,1)S(1)}, u32[]{:S(2)}, u32[]{:S(2)}) async-start(bf16[16,72,128]{2,1,0:T(8,128)(2,1)} %piece.1), calls=%async_computation | async-start | bytes 589824 | tf_op jit(solution)/shard_map/all_to_all | solution.py:278
  18.3 26.4 %collective-permute-start = (bf16[256,2048]{1,0:T(8,128)(2,1)}, bf16[256,2048]{1,0:T(8,128)(2,1)S(1)}, u32[]{:S(2)}, u32[]{:S(2)}) collective-permute-start(bf16[256,2048]{1,0:T(8,128)(2,1)} %bitcast.9), channel_id=1, source_target_pairs={{0,32},{32,0},{64,96},{96,64},{1,33},{33,1},{65,97},{97,65},{2,34}... | collective-permute-start | bytes 3145736 | tf_op jit(solution)/shard_map/ppermute | solution.py:267
  21.8 27.9 %collective-permute-start.1 = (bf16[256,2048]{1,0:T(8,128)(2,1)}, bf16[256,2048]{1,0:T(8,128)(2,1)}, u32[]{:S(2)}, u32[]{:S(2)}) collective-permute-start(bf16[256,2048]{1,0:T(8,128)(2,1)} %bitcast.10), channel_id=1, source_target_pairs={{0,96},{32,64},{64,32},{96,0},{1,97},{33,65},{65,33},{97,1},{2,98}... | collective-permute-start | bytes 3145736 | tf_op jit(solution)/shard_map/ppermute | solution.py:267
  38.2 25.0 %all-to-all-start.1 = ((bf16[4,1152,128]{2,1,0:T(8,128)(2,1)}), bf16[4,1152,128]{2,1,0:T(8,128)(2,1)}, u32[]{:S(2)}, u32[]{:S(2)}) async-start(bf16[4,1152,128]{2,1,0:T(8,128)(2,1)} %tile.9), calls=%async_computation.1 | async-start | bytes 2359296 | tf_op jit(solution)/shard_map/all_to_all | solution.py:279
  42.5 23.2 %copy-start.3 = (f32[4]{0:T(128)S(1)}, f32[4]{0:T(128)}, u32[]{:S(2)}) copy-start(f32[4]{0:T(128)} %param.8) | copy-start | bytes 52
  42.5 25.8 %copy-start = (bf16[1,256,2048]{2,1,0:T(8,128)(2,1)S(1)}, bf16[1,256,2048]{2,1,0:T(8,128)(2,1)}, u32[]{:S(2)}) copy-start(bf16[1,256,2048]{2,1,0:T(8,128)(2,1)} %x_ref.1) | copy-start | bytes 3145732
  44.8 18.4 %collective-permute-start.2 = (bf16[160,2048]{1,0:T(8,128)(2,1)S(1)}, bf16[160,2048]{1,0:T(8,128)(2,1)S(1)}, u32[]{:S(2)}, u32[]{:S(2)}) collective-permute-start(bf16[160,2048]{1,0:T(8,128)(2,1)S(1)} %slice.8), channel_id=1, source_target_pairs={{0,96},{32,64},{64,32},{96,0},{1,97},{33,65},{65,33},{97,1},{2,98}... | collective-permute-start | bytes 1966088 | tf_op jit(solution)/shard_map/ppermute | solution.py:267
  50.7 11.1 %collective-permute-start.3 = (bf16[96,2048]{1,0:T(8,128)(2,1)S(1)}, bf16[96,2048]{1,0:T(8,128)(2,1)S(1)}, u32[]{:S(2)}, u32[]{:S(2)}) collective-permute-start(bf16[96,2048]{1,0:T(8,128)(2,1)S(1)} %slice.9), channel_id=1, source_target_pairs={{0,32},{32,0},{64,96},{96,64},{1,33},{33,1},{65,97},{97,65},{2,34}... | collective-permute-start | bytes 1179656 | tf_op jit(solution)/shard_map/ppermute | solution.py:267
  63.2 5.1 %collective-permute-start.4 = (bf16[4608,128]{1,0:T(8,128)(2,1)}, bf16[4608,128]{1,0:T(8,128)(2,1)}, u32[]{:S(2)}, u32[]{:S(2)}) collective-permute-start(bf16[4608,128]{1,0:T(8,128)(2,1)} %bitcast.6), channel_id=1, source_target_pairs={{0,1},{1,0},{2,3},{3,2},{4,5},{5,4},{6,7},{7,6},{8,9},{9,8},{10,11... | collective-permute-start | bytes 3538952 | tf_op jit(solution)/shard_map/ppermute | solution.py:281
